TPU v7x, 128 devices: a whole 4x4x4 slice. The times are simulated.
128 devices in a mesh: space: 16 (over y, x_hi, core), vec: 8 (over x_lo, z).
Axes of the slice: x: 4 (x_hi: 2, x_lo: 2; x = x_hi * 2 + x_lo), y: 4, z: 4, core: 2. Of those that a mesh axis runs over, the one named last changes fastest.
Arguments:
- vectors: float32 [2, 3, 384, 16, 2048], P(None, None, 'vec', 'space'), may hold values from -0.375 to 0.375
- links: float32 [3, 2, 3, 3, 16, 2048], P(None, None, None, None, 'space'), may hold values from -3.5 to 3.5
- momenta: int32 [2, 3], replicated, may hold values from -2 to 2
- directions: int32 [3], replicated, may hold values from 0 to 2, each once
Outputs:
- elementals: float32 [2, 3, 2, 384, 384], P(None, None, None, 'space', 'vec')
Inputs may be any that keep to these rules, and one draw needn't show every extreme that they name: directions holds each of 0, 1, 2 once.
All inputs are finite; a program needn't handle non-finite values.
Results may differ from a plain program's by a relative error of at most 0.000098.
Values sent between devices are 32-bit elements; how exact they have to be, the bound alone decides.
A program may use at most 128 MiB of HBM per device.

v0:
```python
import jax
import jax.numpy as jnp
from jax import lax
from jax.sharding import PartitionSpec as P

LY = 32
LZ = 64


def padded_2(shard, sides, width):
    for axis, dim in sides:
        size, length = (lax.axis_size(axis), shard.shape[dim])
        up = [(i, (i + 1) % size) for i in range(size)]
        down = [(j, i) for i, j in up]
        last = lax.slice_in_dim(shard, length - width, length, axis=dim)
        first = lax.slice_in_dim(shard, 0, width, axis=dim)
        before = lax.ppermute(last, axis, up)
        after = lax.ppermute(first, axis, down)
        shard = jnp.concatenate([before, shard, after], axis=dim)
    return shard


def shifted(value, axis, steps):
    count = lax.axis_size(axis)
    pairs = [(source, (source + steps) % count) for source in range(count)]
    return lax.ppermute(value, axis, pairs)


def site_shift(field, mu, step, plane_y, plane_z):
    shape = field.shape
    cube = field.reshape(shape[:-1] + (plane_y, plane_z))
    cube = jnp.roll(cube, -step, axis=-3 + mu)
    return cube.reshape(shape)


def color_apply(link, field, dagger):
    link_re = link[0]
    link_im = link[1]
    if dagger:
        link_re = jnp.swapaxes(link_re, 0, 1)
        link_im = -jnp.swapaxes(link_im, 0, 1)
    link_re = link_re[:, :, None]
    link_im = link_im[:, :, None]
    field_re = field[0][None]
    field_im = field[1][None]
    out_re = jnp.sum(link_re * field_re - link_im * field_im, axis=1)
    out_im = jnp.sum(link_re * field_im + link_im * field_re, axis=1)
    return jnp.stack([out_re, out_im], 0)


def phase_tables(momenta, xcoord, sites, extent_x, plane_y, plane_z):
    ycoord = sites // plane_z
    zcoord = sites % plane_z
    p0 = momenta[:, 0][:, None, None]
    p1 = momenta[:, 1][:, None, None]
    p2 = momenta[:, 2][:, None, None]
    frac = (p0 * xcoord % extent_x).astype(jnp.float32) / extent_x
    frac = frac + (p1 * ycoord[None, None] % plane_y).astype(jnp.float32) / plane_y
    frac = frac + (p2 * zcoord[None, None] % plane_z).astype(jnp.float32) / plane_z
    theta = 2.0 * jnp.pi * frac
    return (jnp.cos(theta), jnp.sin(theta))


def elemental_block(left_vecs, right_disp, cosine, sine):
    vec_re = left_vecs[0][None]
    vec_im = left_vecs[1][None]
    cosine = cosine[:, None, None]
    sine = sine[:, None, None]
    left_re = vec_re * cosine - vec_im * sine
    left_im = -(vec_re * sine + vec_im * cosine)
    left = jnp.stack([left_re, left_im], 1)
    gram = jnp.einsum(
        "mpcaxs,dqcbxs->mpadqb",
        left,
        right_disp,
        precision=lax.Precision.HIGHEST,
        preferred_element_type=jnp.float32,
    )
    part_re = gram[:, 0, :, :, 0] - gram[:, 1, :, :, 1]
    part_im = gram[:, 0, :, :, 1] + gram[:, 1, :, :, 0]
    stacked = jnp.stack([part_re, part_im], 1)
    return jnp.transpose(stacked, (0, 3, 1, 2, 4))


def on_device(vectors, links, momenta, directions):
    plane_y = LY
    plane_z = LZ
    extent_x = lax.axis_size("space")
    xcoord = lax.axis_index("space")
    padded = padded_2(vectors, (("space", 3),), 1)
    lower = shifted(links[0], "space", 1)
    forward_x = color_apply(links[0], padded[:, :, :, 2:3], False)
    backward_x = color_apply(lower, padded[:, :, :, 0:1], True)
    displaced_list = [forward_x - backward_x]
    for mu in (1, 2):
        forward = color_apply(links[mu], site_shift(vectors, mu, 1, plane_y, plane_z), False)
        backward = site_shift(color_apply(links[mu], vectors, True), mu, -1, plane_y, plane_z)
        displaced_list.append(forward - backward)
    displaced = jnp.stack(displaced_list, 0)
    site_count = vectors.shape[4]
    sites = jnp.arange(site_count, dtype=jnp.int32)
    cosine, sine = phase_tables(momenta, xcoord, sites, extent_x, plane_y, plane_z)
    block = elemental_block(
        lax.all_gather(vectors, "vec", axis=2, tiled=True), displaced, cosine, sine
    )
    reduced = lax.psum_scatter(block, "space", scatter_dimension=3, tiled=True)
    return jnp.take(reduced, directions, axis=1)


def solution(mesh):
    placed = (
        P(None, None, "vec", "space", None),
        P(None, None, None, None, "space", None),
        P(),
        P(),
    )
    return jax.shard_map(
        on_device,
        mesh=mesh,
        in_specs=placed,
        out_specs=P(None, None, None, "space", "vec"),
        check_vma=False,
    )
```

profile of v0, /device:TPU:0, one launch (start us, length us, event | category | flops | bytes accessed | tf_op | source)
XLA Modules:
  0.0 485.8 jit_solution(10122858625052142215)
XLA Ops:
  8.2 5.0 %collective-permute-start = (f32[2,3,48,1,2048]{4,3,2,1,0:T(1,128)S(1)}, f32[2,3,48,1,2048]{4,3,2,1,0:T(1,128)}, u32[]{:S(2)}, u32[]{:S(2)}) collective-permute-start(f32[2,3,48,1,2048]{4,3,2,1,0:T(1,128)S(1)} %copy-done.1), channel_id=1, source_target_pairs={{8,0},{16,8},{24,16},{32,24},{40,32},{48,40},{56,48},{64,56},{72,6... | collective-permute-start | bytes 7077896 | tf_op jit(solution)/shard_map/ppermute | solution.py:18
  14.8 7.8 %reduce.15 = f32[2,3,48,2048]{3,2,1,0:T(8,128)} reduce(f32[2,3,48,1,2048]{4,3,2,1,0:T(1,128)S(1)} %copy-done.1, f32[]{:T(128)} %constant.107), dimensions={3}, to_apply=%param.4.reduce_sub_computation | reduce | bytes 4718596 | tf_op args[0]
  22.6 5.4 %reshape.755 = f32[2,3,48,1,32,64]{5,4,2,1,0,3:T(8,128)} reshape(f32[2,3,48,2048]{3,2,1,0:T(8,128)} %reduce.15) | data formatting | bytes 4718592 | tf_op jit(solution)/shard_map/reshape | solution.py:31
  28.0 5.6 %slice.189 = f32[2,3,48,1,31,64]{5,4,2,1,0,3:T(8,128)} slice(f32[2,3,48,1,32,64]{5,4,2,1,0,3:T(8,128)} %reshape.755), slice={[0:2], [0:3], [0:48], [0:1], [1:32], [0:64]} | slice | bytes 4571136 | tf_op jit(solution)/shard_map/jit(_roll_static)/slice | solution.py:32
  34.5 3.5 slice.193
  42.3 4.4 subtract_reduce_fusion.2
  49.9 3.2 stack.81
  53.0 5.9 %fusion.8 = f32[2,3,48,1,32,64]{5,4,2,1,0,3:T(8,128)} fusion(f32[1,3,48,1,32,64]{5,4,2,1,0,3:T(8,128)} %bitcast.159, f32[1,3,48,1,32,64]{5,4,2,1,0,3:T(8,128)} %bitcast.158), kind=kLoop, calls=%fused_computation.18 | loop fusion | flops 1769472 | bytes 4718592 | tf_op jit(solution)/shard_map/jit(_roll_static)/concatenate | solution.py:32
  59.0 5.1 %reshape.756 = f32[1,2,3,48,1,2048]{5,3,2,1,0,4:T(8,128)} reshape(f32[2,3,48,1,32,64]{5,4,2,1,0,3:T(8,128)} %fusion.8) | data formatting | bytes 4718592 | tf_op jit(solution)/shard_map/reshape | solution.py:33
  64.1 5.4 %fusion.10 = (f32[1,3,48,1,32,64]{5,4,2,1,0,3:T(8,128)}, f32[1,3,48,1,32,64]{5,4,2,1,0,3:T(8,128)}) fusion(f32[2,3,48,1,31,64]{5,4,2,1,0,3:T(8,128)} %slice.189, f32[2,3,48,1,1,64]{5,4,2,1,0,3:T(1,128)} %slice.190), kind=kLoop, calls=%fused_computation.37 | loop fusion | flops 589824 | bytes 4718592 | tf_op jit(solution)/shard_map/jit(_roll_static)/concatenate | solution.py:32
  75.6 3.2 stack.86
  81.2 3.8 slice_maximum_fusion
  85.0 3.4 fusion.7
  88.4 5.2 %reshape.757 = f32[1,2,3,48,1,2048]{5,3,2,1,0,4:T(8,128)} reshape(f32[2,3,48,1,32,64]{5,4,2,1,0,3:T(8,128)} %fusion.7) | data formatting | bytes 4718592 | tf_op jit(solution)/shard_map/reshape | solution.py:33
  93.6 7.2 %fusion.9 = (f32[1,3,48,1,32,64]{5,4,2,1,0,3:T(8,128)}, f32[1,3,48,1,32,64]{5,4,2,1,0,3:T(8,128)}) fusion(f32[2,3,48,1,32,63]{5,4,2,1,0,3:T(8,128)} %slice.193, f32[2,3,48,1,32,1]{5,4,2,1,0,3:T(8,128)} %bitcast.153), kind=kLoop, calls=%fused_computation.36 | loop fusion | flops 589824 | bytes 4718592 | tf_op jit(solution)/shard_map/jit(_roll_static)/concatenate | solution.py:32
  103.8 3.4 mul.738
  118.9 3.4 fusion.40
  124.4 3.4 fusion.39
  131.5 115.4 %all-gather.2.cloned.1.call-done = f32[2,3,384,1,2048]{4,3,2,1,0:T(1,128)} async-done(((f32[2,3,48,1,2048]{4,3,2,1,0:T(1,128)}), f32[2,3,384,1,2048]{4,3,2,1,0:T(1,128)}) %all-gather.2.cloned.1.call-update) | async-done | bytes 18874384 | tf_op jit(solution)/shard_map/all_gather | solution.py:104
  246.9 13.3 %fusion.38 = (f32[1,3,384,1,2048]{4,3,2,1,0:T(1,128)}, f32[1,3,384,1,2048]{4,3,2,1,0:T(1,128)}) fusion(f32[2,3,384,1,2048]{4,3,2,1,0:T(1,128)} %all-gather.2.cloned.1.call-done), kind=kLoop, calls=%fused_computation.122 | loop fusion | bytes 37748736 | tf_op jit(solution)/shard_map/slice | solution.py:65
  260.2 13.8 %copy_bitcast_fusion = (f32[3,384,2048]{2,1,0:T(8,128)S(1)}, f32[3,384,2048]{2,1,0:T(8,128)S(1)}) fusion(f32[1,3,384,1,2048]{4,3,2,1,0:T(1,128)} %get-tuple-element.25, f32[1,3,384,1,2048]{4,3,2,1,0:T(1,128)} %get-tuple-element.24), kind=kLoop, calls=%fused_computation.7 | loop fusion | bytes 37748736
  274.1 13.2 %multiply_subtract_fusion = (f32[2,1,3,384,1,2048]{5,3,2,1,0,4:T(8,128)}, f32[2,1,3,384,1,2048]{5,3,2,1,0,4:T(8,128)}) fusion(f32[2,2048]{1,0:T(2,128)S(1)} %get-tuple-element.49, f32[3,384,2048]{2,1,0:T(8,128)S(1)} %get-tuple-element.70, f32[2,2048]{1,0:T(2,128)S(1)} %get-tuple-element.48, f32[3,384,2048]{2,1,0:T(8,128)S(1)} %get-tuple-element.71), kind=kLoop, calls=%fused_computation.6 | loop fusion | flops 33030144 | bytes 56655872 | tf_op jit(solution)/shard_map/sub | solution.py:69
  287.3 40.7 %fusion.11 = f32[2,2,384,3,2,48]{2,5,4,3,1,0:T(8,128)S(1)} fusion(f32[1,2,3,48,1,2048]{5,3,2,1,0,4:T(8,128)} %maximum_subtract_fusion.2, f32[1,2,3,48,1,2048]{5,3,2,1,0,4:T(8,128)} %maximum_subtract_fusion.1, f32[1,2,3,48,1,2048]{5,3,2,1,0,4:T(8,128)} %maximum_subtract_fusion, f32[2,1,3,384,1,2048]{5,3,2,1,0,4:T(8,128)} %get-tuple-element.23, ...), kind=kOutput, calls=%fused_computation.43 | convolution fusion | flops 32627884032 | bytes 46596096 | tf_op jit(solution)/shard_map/mpcaxs,dqcbxs->mpadqb/dot_general | solution.py:72
  332.7 143.6 %all-reduce.3.cloned.1.call-done = f32[2,3,2,384,48]{4,2,1,0,3:T(2,128)} async-done(((f32[2,3,2,384,48]{4,2,1,0,3:T(2,128)}), f32[2,3,2,384,48]{4,2,1,0,3:T(2,128)}) %all-reduce.3.cloned.1.call-update) | async-done | bytes 884752
  (85 shorter events, 46.6 us)
Async XLA Ops:
  6.5 1.7 copy-start.1
  6.5 240.4 %all-gather.2.cloned.1.call-start = ((), (), s32[]{:S(2)}) async-start(), calls=%async_computation | async-start | bytes 21233664 | tf_op jit(solution)/shard_map/all_gather | solution.py:104
  7.3 469.0 %all-reduce.3.cloned.1.call-start = ((), (), s32[]{:S(2)}) async-start(), calls=%async_computation.1 | async-start | bytes 4718592
  8.2 110.7 %collective-permute-start = (f32[2,3,48,1,2048]{4,3,2,1,0:T(1,128)S(1)}, f32[2,3,48,1,2048]{4,3,2,1,0:T(1,128)}, u32[]{:S(2)}, u32[]{:S(2)}) collective-permute-start(f32[2,3,48,1,2048]{4,3,2,1,0:T(1,128)S(1)} %copy-done.1), channel_id=1, source_target_pairs={{8,0},{16,8},{24,16},{32,24},{40,32},{48,40},{56,48},{64,56},{72,6... | collective-permute-start | bytes 7077896 | tf_op jit(solution)/shard_map/ppermute | solution.py:18
  13.2 111.2 %collective-permute-start.2 = (f32[2,3,48,1,2048]{4,3,2,1,0:T(1,128)S(1)}, f32[2,3,48,1,2048]{4,3,2,1,0:T(1,128)}, u32[]{:S(2)}, u32[]{:S(2)}) collective-permute-start(f32[2,3,48,1,2048]{4,3,2,1,0:T(1,128)S(1)} %copy-done.1), channel_id=1, source_target_pairs={{0,8},{8,16},{16,24},{24,32},{32,40},{40,48},{48,56},{56,64},{64,7... | collective-permute-start | bytes 7077896 | tf_op jit(solution)/shard_map/ppermute | solution.py:17
  14.8 103.0 %collective-permute-start.1 = (f32[2,3,3,1,2048]{4,3,2,1,0:T(1,128)}, f32[2,3,3,1,2048]{4,3,2,1,0:T(1,128)}, u32[]{:S(2)}, u32[]{:S(2)}) collective-permute-start(f32[2,3,3,1,2048]{4,3,2,1,0:T(1,128)} %slice_bitcast_fusion.2), channel_id=1, source_target_pairs={{0,8},{8,16},{16,24},{24,32},{32,40},{40,48},{48,56},{56,64},{64,7... | collective-permute-start | bytes 442376 | tf_op jit(solution)/shard_map/ppermute | solution.py:26
  28.0 5.6 %copy-start = (f32[2,3,48,1,32,64]{5,4,2,1,0,3:T(8,128)S(1)}, f32[2,3,48,1,32,64]{5,4,2,1,0,3:T(8,128)}, u32[]{:S(2)}) copy-start(f32[2,3,48,1,32,64]{5,4,2,1,0,3:T(8,128)} %reshape.755) | copy-start | bytes 7077892
  34.5 3.5 copy-start.9
  81.2 3.8 copy-start.2
  81.2 3.8 copy-start.3
  103.8 3.4 copy-start.14
  103.8 4.7 copy-start.6
  108.5 2.7 copy-start.12
  108.5 2.7 copy-start.13
  108.5 2.8 copy-start.7
  108.5 2.8 copy-start.8
  111.3 1.7 copy-start.4
  113.0 1.7 copy-start.10
  113.0 1.7 copy-start.11
  113.0 2.6 copy-start.5
  328.2 3.2 copy-start.16
  328.2 4.4 copy-start.15
Sparse Core Ops, SparseCore 0:
  9.0 237.8 all-gather.1
  331.5 144.7 all-reduce.2
where the time goes:
time: 493 us; the launch traced here: 486 us
  waiting for transfers between devices  260 us (53%)
  local copies, waits for them, and re-layouts  101 us (20%)
  other arithmetic  65.1 us (13%)
  matrix products  40.7 us (8%)
  between operations  14.6 us (3%)
  starting transfers between devices  5.04 us (1%)
    unnamed x3, waiting for transfers between devices  144 us
    all_gather x1, waiting for transfers between devices, on_device(): lax.all_gather(vectors, 'vec', axis=2, tiled=True)  115 us
    dot_general x1, matrix products, elemental_block(): jnp.einsum('mpcaxs,dqcbxs->mpadqb', left, right_disp, precision=lax.Preci...  40.7 us
    unnamed x43, local copies, waits for them, and re-layouts  22 us
    concatenate x4, other arithmetic, site_shift(): cube = jnp.roll(cube, -step, axis=-3 + mu)  22 us
    slice x1, local copies, waits for them, and re-layouts, elemental_block(): vec_re = left_vecs[0][None]  13.3 us
    sub x1, other arithmetic, elemental_block(): left_re = vec_re * cosine - vec_im * sine  13.2 us
    mul x7, local copies, waits for them, and re-layouts, color_apply(): out_re = jnp.sum(link_re * field_re - link_im * field_im, axis=1)  12.8 us
  transfers between devices with their start and end apart: 5, of which 2 were waited for; matrix products, arithmetic and copies ran while one was open for 24% of the time, Pallas kernels for 0%

commit v1 on v0

v1 whole, which is shorter than its diff:
```python
import functools

import jax
import jax.numpy as jnp
from jax import lax
from jax.experimental import pallas as pl
from jax.experimental.pallas import tpu as pltpu
from jax.sharding import PartitionSpec as P

MESH = pl.DeviceIdType.MESH
F32 = jnp.float32
BF16 = jnp.bfloat16
VMEM = pl.BlockSpec(memory_space=pltpu.VMEM)
HBM = pl.BlockSpec(memory_space=pl.ANY)


def coords():
    s, k = lax.axis_index("space"), lax.axis_index("vec")
    return s // 4, (s // 2) % 2, s % 2, k // 4, k % 4


def lane_of(shape):
    return lax.broadcasted_iota(jnp.int32, shape, len(shape) - 1)


def exchange_kernel(x_ref, u_ref, v_ref, up_ref, dn_ref, lk_ref, ulo_ref,
                    stage, lstage, send, recv, lsend, lrecv, fsend, frecv, usend, urecv):
    y, xh, c, xl, z = coords()
    s, k = lax.axis_index("space"), lax.axis_index("vec")
    x = xh * 2 + xl
    selfish = c == xh
    q = 2 * y + c
    qn, qp = (q + 1) % 8, (q + 7) % 8
    s_next = (qn // 2 * 2 + xh) * 2 + qn % 2
    s_prev = (qp // 2 * 2 + xh) * 2 + qp % 2

    def target(i):
        xt, zt = (x + i // 4) % 4, (z + i % 4) % 4
        return (y * 2 + xt // 2) * 2 + xh, (xt % 2) * 4 + zt, xt * 4 + zt

    def origin(i):
        return (y * 2 + c) * 2 + i % 2, i // 2

    barrier = pltpu.get_barrier_semaphore()

    def greet(i, _):
        st, kt, _j = target(i)

        @pl.when(jnp.logical_or(st != s, kt != k))
        def _():
            pl.semaphore_signal(barrier, inc=1, device_id=(st, kt), device_id_type=MESH)

        so, ko = origin(i)

        @pl.when(jnp.logical_or(so != s, ko != k))
        def _():
            pl.semaphore_signal(barrier, inc=1, device_id=(so, ko), device_id_type=MESH)

        return 0

    lax.fori_loop(0, 16, greet, 0)
    pl.semaphore_signal(barrier, inc=1, device_id=(s_next, k), device_id_type=MESH)
    pl.semaphore_signal(barrier, inc=1, device_id=(s_prev, k), device_id_type=MESH)

    for xt in range(2):
        j = (xt * 2 + xl) * 4 + z
        lstage[xt, 48:56, :] = jnp.zeros((8, 128), F32)
        lstage[xt, 0:54, :] = u_ref[pl.ds(j, 54, stride=16), :]
    pl.semaphore_wait(barrier, jnp.where(selfish, 32, 34))

    def link_copy(xt):
        return pltpu.make_async_remote_copy(
            src_ref=lstage.at[xt], dst_ref=lk_ref.at[c], send_sem=lsend.at[xt],
            recv_sem=lrecv.at[c], device_id=((y * 2 + xt) * 2 + xh, k), device_id_type=MESH)

    for xt in range(2):
        mine = jnp.logical_and(selfish, xh == xt)

        @pl.when(mine)
        def _():
            pltpu.make_async_copy(lstage.at[xt], lk_ref.at[c], lrecv.at[c]).start()

        @pl.when(jnp.logical_not(mine))
        def _():
            link_copy(xt).start()

    lane = lane_of((144, 128))

    def main_copy(i):
        st, kt, j = target(i)
        return pltpu.make_async_remote_copy(
            src_ref=stage.at[i], dst_ref=v_ref.at[c, k], send_sem=send.at[i],
            recv_sem=recv.at[c * 8 + k], device_id=(st, kt), device_id_type=MESH)

    def put(i, _):
        st, kt, j = target(i)
        nxt = (j + 1) % 16
        stage[i, 0:288, :] = x_ref[pl.ds(j, 288, stride=16), :]
        re = x_ref[pl.ds(nxt, 144, stride=16), :]
        im = x_ref[pl.ds(144 * 16 + nxt, 144, stride=16), :]
        stage[i, 288:432, :] = jnp.where(lane < 64, re, pltpu.roll(im, 64, 1))
        mine = jnp.logical_and(st == s, kt == k)

        @pl.when(mine)
        def _():
            pltpu.make_async_copy(stage.at[i], v_ref.at[c, k], recv.at[c * 8 + k]).start()

        @pl.when(jnp.logical_not(mine))
        def _():
            main_copy(i).start()

        return 0

    lax.fori_loop(0, 16, put, 0)

    for p in range(2):
        pltpu.make_async_copy(lk_ref.at[p], lk_ref.at[p], lrecv.at[p]).wait()
    ulo = pltpu.make_async_remote_copy(
        src_ref=lk_ref.at[1, pl.ds(0, 24)], dst_ref=ulo_ref, send_sem=usend,
        recv_sem=urecv, device_id=(s_next, k), device_id_type=MESH)
    ulo.start()

    def hand(p, vb):
        return pltpu.make_async_remote_copy(
            src_ref=v_ref.at[p, vb, pl.ds(0, 288)],
            dst_ref=(up_ref if p == 0 else dn_ref).at[vb],
            send_sem=fsend.at[p, vb], recv_sem=frecv.at[p, vb],
            device_id=(s_prev if p == 0 else s_next, k), device_id_type=MESH)

    def pass_on(i, _):
        vb = (k // 4 * 4 + i // 4 * 4) % 8 + (z + 4 - i % 4) % 4
        for p in range(2):
            pltpu.make_async_copy(v_ref.at[p, vb], v_ref.at[p, vb], recv.at[p * 8 + vb]).wait()
            hand(p, vb).start()
        return 0

    lax.fori_loop(0, 8, pass_on, 0)

    def finish(i, _):
        for p in range(2):
            hand(p, i).wait_recv()
            hand(p, i).wait_send()
        return 0

    lax.fori_loop(0, 8, finish, 0)
    ulo.wait_recv()
    ulo.wait_send()
    for xt in range(2):

        @pl.when(jnp.logical_not(jnp.logical_and(selfish, xh == xt)))
        def _():
            link_copy(xt).wait_send()

    def sent(i, _):
        st, kt, _j = target(i)

        @pl.when(jnp.logical_or(st != s, kt != k))
        def _():
            main_copy(i).wait_send()

        return 0

    lax.fori_loop(0, 16, sent, 0)


def exchange(vectors, links):
    dma = pltpu.SemaphoreType.DMA
    return pl.pallas_call(
        exchange_kernel,
        out_shape=[
            jax.ShapeDtypeStruct((2, 8, 432, 128), F32),
            jax.ShapeDtypeStruct((8, 288, 128), F32),
            jax.ShapeDtypeStruct((8, 288, 128), F32),
            jax.ShapeDtypeStruct((2, 56, 128), F32),
            jax.ShapeDtypeStruct((24, 128), F32),
        ],
        in_specs=[VMEM, VMEM],
        out_specs=[HBM] * 5,
        scratch_shapes=[
            pltpu.VMEM((16, 432, 128), F32),
            pltpu.VMEM((2, 56, 128), F32),
            dma((16,)), dma((16,)), dma((2,)), dma((2,)),
            dma((2, 8)), dma((2, 8)), dma(()), dma(()),
        ],
        compiler_params=pltpu.CompilerParams(
            collective_id=0, has_side_effects=True, vmem_limit_bytes=24 << 20),
        name="exchange",
    )(vectors.reshape(288 * 16, 128), links.reshape(54 * 16, 128))


def halves(t):
    hi = t.astype(BF16)
    return hi, (t - hi.astype(F32)).astype(BF16)


def apply_link(link, field):
    out = []
    for i in range(3):
        re = im = None
        for j in range(3):
            ur, ui = link(i, j)
            fr, fi = field[j]
            a = ur * fr - ui * fi
            b = ur * fi + ui * fr
            re = a if re is None else re + a
            im = b if im is None else im + b
        out.append((re, im))
    return out


def products_kernel(mom_ref, v_ref, up_ref, dn_ref, lk_ref, ulo_ref, e_ref,
                    left, right, tab):
    y, xh, c, xl, z = coords()
    step = pl.program_id(0)
    m, mu = step // 3, step % 3

    @pl.when(step == 0)
    def _():
        line = (xh * 2 + xl) * 4 + z
        lane1 = lane_of((8, 128))
        low1 = lane1 < 64
        for mm in range(2):
            for place in range(3):
                plane = 4 * y + 2 * c + (jnp.where(low1, 0, 1) if place == 2 else place)
                row = 2 * line + (2 if place == 2 else jnp.where(low1, 0, 1))
                col = lane1 & 63
                n = (((mom_ref[mm, 0] * plane) & 15) * 4 + ((mom_ref[mm, 1] * row) & 31) * 2
                     + ((mom_ref[mm, 2] * col) & 63)) & 63
                theta = n.astype(F32) * (2.0 * jnp.pi / 64)
                tab[mm, place, 0] = jnp.cos(theta)
                tab[mm, place, 1] = jnp.sin(theta)

        rows = 16
        lane = lane_of((rows, 128))
        low = lane < 64
        col = lane & 63

        def group(g, _):
            vb, sub = g // 3, g % 3
            at = pl.multiple_of(g * rows, rows)

            def comp(ref, reim, col_, *lead):
                first = pl.multiple_of(reim * 144 + col_ * 48 + sub * rows, rows)
                return ref[(*lead, vb, pl.ds(first, rows), slice(None))]

            def link(ref, mu_, dagger, *lead):
                def get(i, j):
                    a, b = (j, i) if dagger else (i, j)
                    r = mu_ * 18 + a * 3 + b
                    ur = ref[(*lead, pl.ds(r, 1), slice(None))]
                    ui = ref[(*lead, pl.ds(r + 9, 1), slice(None))]
                    return ur, (-ui if dagger else ui)
                return get

            def put_right(mu_, place, cc, dr, di):
                kk = pl.ds((6 + cc if place == 2 else cc * 2 + place) * 128, 128)
                for i, t in enumerate((dr, di - dr, dr + di)):
                    hi, lo = halves(t)
                    right[mu_, i, 0, pl.ds(at, rows), kk] = hi
                    right[mu_, i, 1, pl.ds(at, rows), kk] = lo

            v = [[(comp(v_ref, 0, cc, p), comp(v_ref, 1, cc, p)) for cc in range(3)] for p in range(2)]
            above = [(comp(up_ref, 0, cc), comp(up_ref, 1, cc)) for cc in range(3)]
            below = [(comp(dn_ref, 0, cc), comp(dn_ref, 1, cc)) for cc in range(3)]
            packed = []
            for p in range(2):
                packed.append([
                    v_ref[p, vb, pl.ds(pl.multiple_of(288 + cc * 48 + sub * rows, rows), rows), :]
                    for cc in range(3)])
            ext = [
                (jnp.where(low, packed[0][cc], pltpu.roll(packed[1][cc], 64, 1)),
                 jnp.where(low, pltpu.roll(packed[0][cc], 64, 1), packed[1][cc]))
                for cc in range(3)]

            for mm in range(2):
                for place in range(3):
                    co, si = tab[mm, place, 0, 0:1], tab[mm, place, 1, 0:1]
                    for cc in range(3):
                        vr, vi = ext[cc] if place == 2 else v[place][cc]
                        lr = vr * co - vi * si
                        li = -(vr * si + vi * co)
                        kk = pl.ds((6 + cc if place == 2 else cc * 2 + place) * 128, 128)
                        for i, t in enumerate((lr + li, lr, li)):
                            hi, lo = halves(t)
                            left[mm, i, 0, pl.ds(at, rows), kk] = hi
                            left[mm, i, 1, pl.ds(at, rows), kk] = lo

            spill = []
            for p in range(2):
                fwd = apply_link(link(lk_ref, 0, False, p), v[1] if p == 0 else above)
                bwd = (apply_link(link(ulo_ref, 0, True), below) if p == 0
                       else apply_link(link(lk_ref, 0, True, 0), v[0]))
                for cc in range(3):
                    put_right(0, p, cc, fwd[cc][0] - bwd[cc][0], fwd[cc][1] - bwd[cc][1])
                shifted = []
                for cc in range(3):
                    vr, vi = v[p][cc]
                    shifted.append((
                        pltpu.roll(jnp.where(low, packed[p][cc], vr), 64, 1),
                        jnp.where(low, pltpu.roll(vi, 64, 1), packed[p][cc])))
                fwd = apply_link(link(lk_ref, 1, False, p), shifted)
                bwd = apply_link(link(lk_ref, 1, True, p), v[p])
                turned = []
                for cc in range(3):
                    tr, ti = pltpu.roll(bwd[cc][0], 64, 1), pltpu.roll(bwd[cc][1], 64, 1)
                    turned.append((tr, ti))
                    put_right(1, p, cc, fwd[cc][0] - jnp.where(low, 0.0, tr),
                              fwd[cc][1] - jnp.where(low, 0.0, ti))
                spill.append((bwd, turned))
                def ahead(t):
                    return jnp.where(col == 63, pltpu.roll(t, 63, 1), pltpu.roll(t, 127, 1))

                def behind(t):
                    return jnp.where(col == 0, pltpu.roll(t, 65, 1), pltpu.roll(t, 1, 1))

                fwd = apply_link(link(lk_ref, 2, False, p), [(ahead(a), ahead(b)) for a, b in v[p]])
                bwd = apply_link(link(lk_ref, 2, True, p), v[p])
                for cc in range(3):
                    put_right(2, p, cc, fwd[cc][0] - behind(bwd[cc][0]),
                              fwd[cc][1] - behind(bwd[cc][1]))
            for cc in range(3):
                put_right(1, 2, cc,
                          -jnp.where(low, spill[0][1][cc][0], spill[1][0][cc][0]),
                          -jnp.where(low, spill[0][1][cc][1], spill[1][0][cc][1]))
            return 0

        lax.fori_loop(0, 24, group, 0)

    def product(depth):
        dims = (((1,), (1,)), ((), ()))

        def one(i):
            d = pl.ds(0, depth)
            lh, ll = left[m, i, 0, :, d], left[m, i, 1, :, d]
            rh, rl = right[mu, i, 0, :, d], right[mu, i, 1, :, d]
            dot = functools.partial(lax.dot_general, dimension_numbers=dims, preferred_element_type=F32)
            return dot(lh, rh) + dot(lh, rl) + dot(ll, rh)

        k1 = one(0)
        e_ref[0, 1] = k1 + one(1)
        e_ref[0, 0] = k1 - one(2)

    @pl.when(mu == 1)
    def _():
        product(1152)

    @pl.when(mu != 1)
    def _():
        product(768)


def products(momenta, v, up, dn, lk, ulo):
    once = pl.Buffered(1)
    whole = lambda a: pl.BlockSpec(a.shape, lambda i: (0,) * a.ndim, pipeline_mode=once)
    return pl.pallas_call(
        products_kernel,
        grid=(6,),
        out_shape=jax.ShapeDtypeStruct((6, 2, 384, 384), F32),
        in_specs=[pl.BlockSpec(memory_space=pltpu.SMEM)] + [whole(a) for a in (v, up, dn, lk, ulo)],
        out_specs=pl.BlockSpec((1, 2, 384, 384), lambda i: (i, 0, 0, 0)),
        scratch_shapes=[
            pltpu.VMEM((2, 3, 2, 384, 1152), BF16),
            pltpu.VMEM((3, 3, 2, 384, 1152), BF16),
            pltpu.VMEM((2, 3, 2, 8, 128), F32),
        ],
        compiler_params=pltpu.CompilerParams(vmem_limit_bytes=56 << 20),
        cost_estimate=pl.CostEstimate(flops=2 * 18 * 3 * 384 * 384 * 896, bytes_accessed=13 << 20, transcendentals=0),
        name="products",
    )(momenta, v, up, dn, lk, ulo)


def sums_kernel(e_ref, out_ref, cin, cs, yin, ys, xin, xs, zst, zin, zs, lin,
                csend, crecv, asend, arecv, bsend, brecv, zsend, zrecv, lsend, lrecv):
    y, xh, c, xl, z = coords()
    s, k = lax.axis_index("space"), lax.axis_index("vec")
    x = xh * 2 + xl

    def dev(y_, x_, c_, z_):
        return (y_ * 2 + x_ // 2) * 2 + c_, (x_ % 2) * 4 + z_

    def on_y(d):
        return dev((y + d) % 4, x, c, z)

    def on_x(d):
        return dev(y, (x + d) % 4, c, z)

    def on_z(d):
        return dev(y, x, c, (z + d) % 4)

    partner = dev(y, x, 1 - c, z)
    twin = dev(y, xh * 2 + 1 - xl, c, z)
    barrier = pltpu.get_barrier_semaphore()
    pl.semaphore_signal(barrier, inc=1, device_id=partner, device_id_type=MESH)
    for d in (1, 2, 3):
        for on in (on_y, on_x, on_z):
            pl.semaphore_signal(barrier, inc=1, device_id=on(d), device_id_type=MESH)
    pl.semaphore_wait(barrier, 10)

    def core_copy(b):
        return pltpu.make_async_remote_copy(
            src_ref=e_ref.at[b, :, :, 1 - c], dst_ref=cin.at[b], send_sem=csend.at[b],
            recv_sem=crecv.at[b], device_id=partner, device_id_type=MESH)

    for b in range(6):
        core_copy(b).start()

    def first(b, d):
        if b % 2 == 0:
            yt = (y + d) % 4
            src, to = cs.at[b, :, yt], on_y(d)
            dst = yin.at[b // 2, d - 1]
        else:
            xt = (x + d) % 4
            src, to = cs.at[b, xt % 2, :, xt // 2], on_x(d)
            dst = xin.at[b // 2, d - 1]
        return pltpu.make_async_remote_copy(
            src_ref=src, dst_ref=dst, send_sem=asend.at[b, d - 1],
            recv_sem=arecv.at[b, d - 1], device_id=to, device_id_type=MESH)

    def second(b, d):
        if b % 2 == 0:
            xt = (x + d) % 4
            src, to = ys.at[b // 2, xt % 2, xt // 2], on_x(d)
        else:
            src, to = xs.at[b // 2, (y + d) % 4], on_y(d)
        return pltpu.make_async_remote_copy(
            src_ref=src, dst_ref=lin.at[b, d - 1], send_sem=bsend.at[b, d - 1],
            recv_sem=brecv.at[b, d - 1], device_id=to, device_id_type=MESH)

    def third(d):
        return pltpu.make_async_remote_copy(
            src_ref=zst.at[d], dst_ref=zin.at[d - 1], send_sem=zsend.at[d - 1],
            recv_sem=zrecv.at[d - 1], device_id=on_z(d), device_id_type=MESH)

    last = pltpu.make_async_remote_copy(
        src_ref=zs.at[0], dst_ref=zs.at[1], send_sem=lsend, recv_sem=lrecv,
        device_id=twin, device_id_type=MESH)

    for b in range(6):
        core_copy(b).wait_recv()
        for ri in range(2):
            def add(i, _):
                cs[b, ri, i // 2, i % 2] = e_ref[b, ri, i, c] + cin[b, ri, i]
                return 0
            lax.fori_loop(0, 8, add, 0)
        for d in (1, 2, 3):
            first(b, d).start()

    for b in range(6):
        for d in (1, 2, 3):
            first(b, d).wait_recv()
        if b % 2 == 0:
            for ri in range(2):
                for h in range(2):
                    ys[b // 2, ri, h] = (cs[b, ri, y, h] + yin[b // 2, 0, ri, h]) + (
                        yin[b // 2, 1, ri, h] + yin[b // 2, 2, ri, h])
        else:
            for i in range(4):
                xs[b // 2, i] = (cs[b, xl, i, xh] + xin[b // 2, 0, i]) + (
                    xin[b // 2, 1, i] + xin[b // 2, 2, i])
        for d in (1, 2, 3):
            second(b, d).start()

    for b in range(6):
        for d in (1, 2, 3):
            second(b, d).wait_recv()
        own = ys[b // 2, xl, xh] if b % 2 == 0 else xs[b // 2, y]
        t = (own + lin[b, 0]) + (lin[b, 1] + lin[b, 2])
        for d in range(4):
            zt = (z + d) % 4
            zst[d, b] = jnp.where(
                lane_of((24, 128)) < 48,
                pltpu.roll(t, (384 - 48 * zt) % 384, 1)[:, 0:128],
                pltpu.roll(t, (624 - 48 * zt) % 384, 1)[:, 0:128])
    for d in (1, 2, 3):
        third(d).start()
    for d in (1, 2, 3):
        third(d).wait_recv()
    zs[0] = (zst[0] + zin[0]) + (zin[1] + zin[2])
    last.start()
    last.wait_recv()
    for b in range(6):
        own = pltpu.roll(zs[0, b], (128 - 48 * xl) % 128, 1)[:, 0:48]
        other = pltpu.roll(zs[1, b], (128 - 48 * xl) % 128, 1)[:, 0:48]
        out_ref[b, xl] = own
        out_ref[b, 1 - xl] = other
    last.wait_send()
    for d in (1, 2, 3):
        third(d).wait_send()
    for b in range(6):
        core_copy(b).wait_send()
        for d in (1, 2, 3):
            first(b, d).wait_send()
            second(b, d).wait_send()


def sums(e):
    dma = pltpu.SemaphoreType.DMA
    return pl.pallas_call(
        sums_kernel,
        out_shape=jax.ShapeDtypeStruct((6, 2, 24, 48), F32),
        in_specs=[VMEM],
        out_specs=VMEM,
        scratch_shapes=[
            pltpu.VMEM((6, 2, 8, 24, 384), F32),
            pltpu.VMEM((6, 2, 4, 2, 24, 384), F32),
            pltpu.VMEM((3, 3, 2, 2, 24, 384), F32),
            pltpu.VMEM((3, 2, 2, 24, 384), F32),
            pltpu.VMEM((3, 3, 4, 24, 384), F32),
            pltpu.VMEM((3, 4, 24, 384), F32),
            pltpu.VMEM((4, 6, 24, 128), F32),
            pltpu.VMEM((3, 6, 24, 128), F32),
            pltpu.VMEM((2, 6, 24, 128), F32),
            pltpu.VMEM((6, 3, 24, 384), F32),
            dma((6,)), dma((6,)), dma((6, 3)), dma((6, 3)), dma((6, 3)), dma((6, 3)),
            dma((3,)), dma((3,)), dma(()), dma(()),
        ],
        compiler_params=pltpu.CompilerParams(
            collective_id=1, has_side_effects=True, vmem_limit_bytes=48 << 20),
        name="sums",
    )(e.reshape(6, 2, 8, 2, 24, 384))


def on_device(vectors, links, momenta, directions):
    e = products(momenta, *exchange(vectors, links))
    out = sums(e).reshape(2, 3, 2, 24, 48)
    picked = []
    for n in range(3):
        d = directions[n]
        picked.append(jnp.where(d == 0, out[:, 0], jnp.where(d == 1, out[:, 1], out[:, 2])))
    return jnp.stack(picked, axis=1)


def solution(mesh):
    placed = (
        P(None, None, "vec", "space", None),
        P(None, None, None, None, "space", None),
        P(),
        P(),
    )
    return jax.shard_map(
        on_device,
        mesh=mesh,
        in_specs=placed,
        out_specs=P(None, None, None, "space", "vec"),
        check_vma=False,
    )
```

time: 493 us -> 176 us (0.36); the launches traced: 486 us -> 175 us
  waiting for transfers between devices: 260 us -> 0 us
  Pallas kernels: 0 us -> 162 us
  local copies, waits for them, and re-layouts: 101 us -> 8.44 us
  other arithmetic: 65.1 us -> 0.69 us
  matrix products: 40.7 us -> 0 us
  between operations: 14.6 us -> 3.88 us
  starting transfers between devices: 5.04 us -> 0 us
    pallas_call x0 -> x3, Pallas kernels: none -> 162 us  [the longest x1 74.9 us: exchange(): pl.pallas_call(exchange_kernel, out_shape=[jax.ShapeDtypeStruct((2, 8, 43...]
    unnamed x3 -> x0, waiting for transfers between devices: 144 us -> none
    all_gather x1 -> x0, waiting for transfers between devices: 115 us -> none  [on_device(): lax.all_gather(vectors, 'vec', axis=2, tiled=True)]
    dot_general x1 -> x0, matrix products: 40.7 us -> none  [elemental_block(): jnp.einsum('mpcaxs,dqcbxs->mpadqb', left, right_disp, precision=lax.Preci...]
    slice x7 -> x1, local copies, waits for them, and re-layouts: 32.1 us -> 0.62 us  [on_device(): d = directions[n]]
    concatenate x4 -> x0, other arithmetic: 22 us -> none  [site_shift(): cube = jnp.roll(cube, -step, axis=-3 + mu)]
    sub x5 -> x0, other arithmetic: 18.6 us -> none  [the longest x1 13.2 us: elemental_block(): left_re = vec_re * cosine - vec_im * sine]
    reshape x3 -> x0, local copies, waits for them, and re-layouts: 15.7 us -> none  [the longest x2 10.3 us: site_shift(): return cube.reshape(shape)]
  transfers between devices with their start and end apart: 5 -> 0, of which waited for: 2 -> 0; matrix products, arithmetic and copies ran while one was open for 24% -> 0% of each run, Pallas kernels for 0% -> 0%
where the time goes in v1:
time: 176 us; the launch traced here: 175 us
  Pallas kernels  162 us (92%)
  local copies, waits for them, and re-layouts  8.44 us (5%)
  between operations  3.88 us (2%)
    pallas_call x1, Pallas kernels, exchange(): pl.pallas_call(exchange_kernel, out_shape=[jax.ShapeDtypeStruct((2, 8, 43...  74.9 us
    pallas_call x1, Pallas kernels, sums(): pl.pallas_call(sums_kernel, out_shape=jax.ShapeDtypeStruct((6, 2, 24, 48)...  50.3 us
    pallas_call x1, Pallas kernels, products(): pl.pallas_call(products_kernel, grid=(6,), out_shape=jax.ShapeDtypeStruct...  36.6 us
    unnamed x16, local copies, waits for them, and re-layouts  7.82 us

profile of v1, /device:TPU:0, one launch (start us, length us, event | category | flops | bytes accessed | tf_op | source)
XLA Modules:
  0.0 174.8 jit_solution(14974000177266290022)
XLA Ops:
  0.0 0.0 copy-start
  0.0 1.7 copy-done
  1.7 0.0 copy-start.1
  1.7 1.0 copy-done.1
  2.7 74.9 %exchange.1 = (f32[2,8,432,128]{3,2,1,0:T(8,128)S(1)}, f32[8,288,128]{2,1,0:T(8,128)S(1)}, f32[8,288,128]{2,1,0:T(8,128)S(1)}, f32[2,56,128]{2,1,0:T(8,128)S(1)}, f32[24,128]{1,0:T(8,128)S(1)}) custom-call(f32[4608,128]{1,0:T(8,128)S(1)} %bitcast.10, f32[864,128]{1,0:T(8,128)S(1)} %bitcast.12), custom_call_target="tpu_custom_call" | custom-call | tf_op jit(solution)/shard_map/exchange/pallas_call | solution.py:168
  77.6 0.0 copy-start.2
  77.6 1.8 %copy-done.2 = f32[2,8,432,128]{3,2,1,0:T(8,128)} copy-done((f32[2,8,432,128]{3,2,1,0:T(8,128)}, f32[2,8,432,128]{3,2,1,0:T(8,128)S(1)}, u32[]{:S(2)}) %copy-start.2) | copy-done | bytes 3538968
  79.4 0.0 copy-start.3
  79.4 1.0 copy-done.3
  80.4 0.0 copy-start.4
  80.5 1.0 copy-done.4
  81.5 0.0 copy-start.5
  81.5 0.6 copy-done.5
  82.1 0.0 copy-start.6
  82.1 0.6 copy-done.6
  82.7 36.6 %products.1 = f32[6,2,384,384]{3,2,1,0:T(8,128)} custom-call(s32[2,3]{1,0:T(2,128)} %mom_ref.1, f32[2,8,432,128]{3,2,1,0:T(8,128)} %copy-done.2, f32[8,288,128]{2,1,0:T(8,128)} %copy-done.3, f32[8,288,128]{2,1,0:T(8,128)} %copy-done.4, f32[2,56,128]{2,1,0:T(8,128)} %copy-done.5, f32[24,128]{1,0:T(8,128)} %copy-done.6), custom_call_target="tpu_custom_call" | custom-call | flops 14269022208 | bytes 13631488 | tf_op jit(solution)/shard_map/products/pallas_call | solution.py:355
  119.3 0.0 copy-start.7
  119.3 50.3 %sums.1 = f32[6,2,24,48]{3,2,1,0:T(8,128)S(1)} custom-call(f32[6,2,8,2,24,384]{5,4,3,2,1,0:T(8,128)} %bitcast.13), custom_call_target="tpu_custom_call" | custom-call | tf_op jit(solution)/shard_map/sums/pallas_call | solution.py:499
  169.6 0.0 copy-done.7
  169.6 0.6 fusion
  174.1 0.7 pad_maximum_fusion
  (1 shorter events, 0.0 us)
Async XLA Ops:
  0.0 1.7 copy-start
  1.7 1.0 copy-start.1
  77.6 1.9 %copy-start.2 = (f32[2,8,432,128]{3,2,1,0:T(8,128)}, f32[2,8,432,128]{3,2,1,0:T(8,128)S(1)}, u32[]{:S(2)}) copy-start(f32[2,8,432,128]{3,2,1,0:T(8,128)S(1)} %get-tuple-element.10.v_ref) | copy-start | bytes 10616836
  79.4 1.0 copy-start.3
  80.4 1.1 copy-start.4
  81.5 0.6 copy-start.5
  82.1 0.6 copy-start.6
  119.3 50.3 %copy-start.7 = (s32[3]{0:T(128)S(1)}, s32[3]{0:T(128)}, u32[]{:S(2)}) copy-start(s32[3]{0:T(128)} %param.7) | copy-start | bytes 40

commit v2 on v1

v2 whole, which is shorter than its diff:
```python
import functools

import jax
import jax.numpy as jnp
from jax import lax
from jax.experimental import pallas as pl
from jax.experimental.pallas import tpu as pltpu
from jax.sharding import PartitionSpec as P

MESH = pl.DeviceIdType.MESH
F32 = jnp.float32
BF16 = jnp.bfloat16
VMEM = pl.BlockSpec(memory_space=pltpu.VMEM)
HBM = pl.BlockSpec(memory_space=pl.ANY)


def coords():
    s, k = lax.axis_index("space"), lax.axis_index("vec")
    return s // 4, (s // 2) % 2, s % 2, k // 4, k % 4


def lane_of(shape):
    return lax.broadcasted_iota(jnp.int32, shape, len(shape) - 1)


STEPS = ((2, 2), (1, 2), (3, 2), (2, 1), (2, 3), (1, 1), (3, 3), (1, 3),
         (3, 1), (2, 0), (0, 2), (0, 1), (0, 3), (1, 0), (3, 0), (0, 0))


def exchange_kernel(x_ref, u_ref, v_ref, up_ref, dn_ref, lk_ref, ulo_ref,
                    stage, lstage, send, recv, lsend, lrecv, fsend, frecv, usend, urecv):
    y, xh, c, xl, z = coords()
    s, k = lax.axis_index("space"), lax.axis_index("vec")
    x = xh * 2 + xl
    selfish = c == xh
    q = 2 * y + c
    qn, qp = (q + 1) % 8, (q + 7) % 8
    s_next = (qn // 2 * 2 + xh) * 2 + qn % 2
    s_prev = (qp // 2 * 2 + xh) * 2 + qp % 2

    def target(i):
        xt, zt = (x + STEPS[i][0]) % 4, (z + STEPS[i][1]) % 4
        return (y * 2 + xt // 2) * 2 + xh, (xt % 2) * 4 + zt, xt * 4 + zt

    def origin(i):
        return (y * 2 + c) * 2 + i % 2, i // 2

    barrier = pltpu.get_barrier_semaphore()

    def greet(i):
        st, kt, _j = target(i)

        @pl.when(jnp.logical_or(st != s, kt != k))
        def _():
            pl.semaphore_signal(barrier, inc=1, device_id=(st, kt), device_id_type=MESH)

        so, ko = origin(i)

        @pl.when(jnp.logical_or(so != s, ko != k))
        def _():
            pl.semaphore_signal(barrier, inc=1, device_id=(so, ko), device_id_type=MESH)

    for i in range(16):
        greet(i)
    pl.semaphore_signal(barrier, inc=1, device_id=(s_next, k), device_id_type=MESH)
    pl.semaphore_signal(barrier, inc=1, device_id=(s_prev, k), device_id_type=MESH)

    for xt in range(2):
        j = (xt * 2 + xl) * 4 + z
        lstage[xt, 48:56, :] = jnp.zeros((8, 128), F32)
        lstage[xt, 0:54, :] = u_ref[pl.ds(j, 54, stride=16), :]
    pl.semaphore_wait(barrier, jnp.where(selfish, 32, 34))

    def link_copy(xt):
        return pltpu.make_async_remote_copy(
            src_ref=lstage.at[xt], dst_ref=lk_ref.at[c], send_sem=lsend.at[xt],
            recv_sem=lrecv.at[c], device_id=((y * 2 + xt) * 2 + xh, k), device_id_type=MESH)

    for xt in range(2):
        mine = jnp.logical_and(selfish, xh == xt)

        @pl.when(mine)
        def _():
            pltpu.make_async_copy(lstage.at[xt], lk_ref.at[c], lrecv.at[c]).start()

        @pl.when(jnp.logical_not(mine))
        def _():
            link_copy(xt).start()

    lane = lane_of((144, 128))

    def main_copy(i):
        st, kt, j = target(i)
        return pltpu.make_async_remote_copy(
            src_ref=stage.at[i], dst_ref=v_ref.at[c, k], send_sem=send.at[i],
            recv_sem=recv.at[c * 8 + k], device_id=(st, kt), device_id_type=MESH)

    def put(i):
        st, kt, j = target(i)
        nxt = (j + 1) % 16
        stage[i, 0:288, :] = x_ref[pl.ds(j, 288, stride=16), :]
        re = x_ref[pl.ds(nxt, 144, stride=16), :]
        im = x_ref[pl.ds(144 * 16 + nxt, 144, stride=16), :]
        stage[i, 288:432, :] = jnp.where(lane < 64, re, pltpu.roll(im, 64, 1))
        mine = jnp.logical_and(st == s, kt == k)

        @pl.when(mine)
        def _():
            pltpu.make_async_copy(stage.at[i], v_ref.at[c, k], recv.at[c * 8 + k]).start()

        @pl.when(jnp.logical_not(mine))
        def _():
            main_copy(i).start()

    for i in range(16):
        put(i)

    for p in range(2):
        pltpu.make_async_copy(lk_ref.at[p], lk_ref.at[p], lrecv.at[p]).wait()
    ulo = pltpu.make_async_remote_copy(
        src_ref=lk_ref.at[1, pl.ds(0, 24)], dst_ref=ulo_ref, send_sem=usend,
        recv_sem=urecv, device_id=(s_next, k), device_id_type=MESH)
    ulo.start()

    def hand(p, vb):
        return pltpu.make_async_remote_copy(
            src_ref=v_ref.at[p, vb, pl.ds(0, 288)],
            dst_ref=(up_ref if p == 0 else dn_ref).at[vb],
            send_sem=fsend.at[p, vb], recv_sem=frecv.at[p, vb],
            device_id=(s_prev if p == 0 else s_next, k), device_id_type=MESH)

    def pass_on(i):
        xs, zs = (x + 4 - STEPS[i][0]) % 4, (z + 4 - STEPS[i][1]) % 4
        vb = (xs % 2) * 4 + zs

        @pl.when(xs // 2 == c)
        def _():
            for p in range(2):
                pltpu.make_async_copy(v_ref.at[p, vb], v_ref.at[p, vb], recv.at[p * 8 + vb]).wait()
                hand(p, vb).start()

    for i in range(16):
        pass_on(i)

    def finish(i, _):
        for p in range(2):
            hand(p, i).wait_recv()
            hand(p, i).wait_send()
        return 0

    lax.fori_loop(0, 8, finish, 0)
    ulo.wait_recv()
    ulo.wait_send()
    for xt in range(2):

        @pl.when(jnp.logical_not(jnp.logical_and(selfish, xh == xt)))
        def _():
            link_copy(xt).wait_send()

    def sent(i):
        st, kt, _j = target(i)

        @pl.when(jnp.logical_or(st != s, kt != k))
        def _():
            main_copy(i).wait_send()

    for i in range(16):
        sent(i)


def exchange(vectors, links):
    dma = pltpu.SemaphoreType.DMA
    return pl.pallas_call(
        exchange_kernel,
        out_shape=[
            jax.ShapeDtypeStruct((2, 8, 432, 128), F32),
            jax.ShapeDtypeStruct((8, 288, 128), F32),
            jax.ShapeDtypeStruct((8, 288, 128), F32),
            jax.ShapeDtypeStruct((2, 56, 128), F32),
            jax.ShapeDtypeStruct((24, 128), F32),
        ],
        in_specs=[VMEM, VMEM],
        out_specs=[HBM] * 5,
        scratch_shapes=[
            pltpu.VMEM((16, 432, 128), F32),
            pltpu.VMEM((2, 56, 128), F32),
            dma((16,)), dma((16,)), dma((2,)), dma((2,)),
            dma((2, 8)), dma((2, 8)), dma(()), dma(()),
        ],
        compiler_params=pltpu.CompilerParams(
            collective_id=0, has_side_effects=True, vmem_limit_bytes=24 << 20),
        name="exchange",
    )(vectors.reshape(288 * 16, 128), links.reshape(54 * 16, 128))


def halves(t):
    hi = t.astype(BF16)
    return hi, (t - hi.astype(F32)).astype(BF16)


def apply_link(link, field):
    out = []
    for i in range(3):
        re = im = None
        for j in range(3):
            ur, ui = link(i, j)
            fr, fi = field[j]
            a = ur * fr - ui * fi
            b = ur * fi + ui * fr
            re = a if re is None else re + a
            im = b if im is None else im + b
        out.append((re, im))
    return out


def elementals_kernel(mom_ref, v_ref, up_ref, dn_ref, lk_ref, ulo_ref, out_ref,
                      left, right, tab, e_ref, cin, cs, yin, ys, xin, xs, zst, zin, zs, lin,
                      csend, crecv, asend, arecv, bsend, brecv, zsend, zrecv, lsend, lrecv):
    y, xh, c, xl, z = coords()
    x = xh * 2 + xl

    def dev(y_, x_, c_, z_):
        return (y_ * 2 + x_ // 2) * 2 + c_, (x_ % 2) * 4 + z_

    def on_y(d):
        return dev((y + d) % 4, x, c, z)

    def on_x(d):
        return dev(y, (x + d) % 4, c, z)

    def on_z(d):
        return dev(y, x, c, (z + d) % 4)

    partner = dev(y, x, 1 - c, z)
    twin = dev(y, xh * 2 + 1 - xl, c, z)
    barrier = pltpu.get_barrier_semaphore()
    pl.semaphore_signal(barrier, inc=1, device_id=partner, device_id_type=MESH)
    for d in (1, 2, 3):
        for on in (on_y, on_x, on_z):
            pl.semaphore_signal(barrier, inc=1, device_id=on(d), device_id_type=MESH)

    line = (xh * 2 + xl) * 4 + z
    lane1 = lane_of((8, 128))
    low1 = lane1 < 64
    for mm in range(2):
        for place in range(3):
            plane = 4 * y + 2 * c + (jnp.where(low1, 0, 1) if place == 2 else place)
            row = 2 * line + (2 if place == 2 else jnp.where(low1, 0, 1))
            col = lane1 & 63
            n = (((mom_ref[mm, 0] * plane) & 15) * 4 + ((mom_ref[mm, 1] * row) & 31) * 2
                 + ((mom_ref[mm, 2] * col) & 63)) & 63
            theta = n.astype(F32) * (2.0 * jnp.pi / 64)
            tab[mm, place, 0] = jnp.cos(theta)
            tab[mm, place, 1] = jnp.sin(theta)

    rows = 16
    lane = lane_of((rows, 128))
    low = lane < 64
    col = lane & 63

    def group(g, _):
        vb, sub = g // 3, g % 3
        at = pl.multiple_of(g * rows, rows)

        def comp(ref, reim, col_, *lead):
            first = pl.multiple_of(reim * 144 + col_ * 48 + sub * rows, rows)
            return ref[(*lead, vb, pl.ds(first, rows), slice(None))]

        def link(ref, mu_, dagger, *lead):
            def get(i, j):
                a, b = (j, i) if dagger else (i, j)
                r = mu_ * 18 + a * 3 + b
                ur = ref[(*lead, pl.ds(r, 1), slice(None))]
                ui = ref[(*lead, pl.ds(r + 9, 1), slice(None))]
                return ur, (-ui if dagger else ui)
            return get

        def put_right(mu_, place, cc, dr, di):
            kk = pl.ds((6 + cc if place == 2 else cc * 2 + place) * 128, 128)
            for i, t in enumerate((dr, di - dr, dr + di)):
                hi, lo = halves(t)
                right[mu_, i, 0, pl.ds(at, rows), kk] = hi
                right[mu_, i, 1, pl.ds(at, rows), kk] = lo

        v = [[(comp(v_ref, 0, cc, p), comp(v_ref, 1, cc, p)) for cc in range(3)] for p in range(2)]
        above = [(comp(up_ref, 0, cc), comp(up_ref, 1, cc)) for cc in range(3)]
        below = [(comp(dn_ref, 0, cc), comp(dn_ref, 1, cc)) for cc in range(3)]
        packed = []
        for p in range(2):
            packed.append([
                v_ref[p, vb, pl.ds(pl.multiple_of(288 + cc * 48 + sub * rows, rows), rows), :]
                for cc in range(3)])
        ext = [
            (jnp.where(low, packed[0][cc], pltpu.roll(packed[1][cc], 64, 1)),
             jnp.where(low, pltpu.roll(packed[0][cc], 64, 1), packed[1][cc]))
            for cc in range(3)]

        for mm in range(2):
            for place in range(3):
                co, si = tab[mm, place, 0, 0:1], tab[mm, place, 1, 0:1]
                for cc in range(3):
                    vr, vi = ext[cc] if place == 2 else v[place][cc]
                    lr = vr * co - vi * si
                    li = -(vr * si + vi * co)
                    kk = pl.ds((6 + cc if place == 2 else cc * 2 + place) * 128, 128)
                    for i, t in enumerate((lr + li, lr, li)):
                        hi, lo = halves(t)
                        left[mm, i, 0, pl.ds(at, rows), kk] = hi
                        left[mm, i, 1, pl.ds(at, rows), kk] = lo

        spill = []
        for p in range(2):
            fwd = apply_link(link(lk_ref, 0, False, p), v[1] if p == 0 else above)
            bwd = (apply_link(link(ulo_ref, 0, True), below) if p == 0
                   else apply_link(link(lk_ref, 0, True, 0), v[0]))
            for cc in range(3):
                put_right(0, p, cc, fwd[cc][0] - bwd[cc][0], fwd[cc][1] - bwd[cc][1])
            shifted = []
            for cc in range(3):
                vr, vi = v[p][cc]
                shifted.append((
                    pltpu.roll(jnp.where(low, packed[p][cc], vr), 64, 1),
                    jnp.where(low, pltpu.roll(vi, 64, 1), packed[p][cc])))
            fwd = apply_link(link(lk_ref, 1, False, p), shifted)
            bwd = apply_link(link(lk_ref, 1, True, p), v[p])
            turned = []
            for cc in range(3):
                tr, ti = pltpu.roll(bwd[cc][0], 64, 1), pltpu.roll(bwd[cc][1], 64, 1)
                turned.append((tr, ti))
                put_right(1, p, cc, fwd[cc][0] - jnp.where(low, 0.0, tr),
                          fwd[cc][1] - jnp.where(low, 0.0, ti))
            spill.append((bwd, turned))
            def ahead(t):
                return jnp.where(col == 63, pltpu.roll(t, 63, 1), pltpu.roll(t, 127, 1))

            def behind(t):
                return jnp.where(col == 0, pltpu.roll(t, 65, 1), pltpu.roll(t, 1, 1))

            fwd = apply_link(link(lk_ref, 2, False, p), [(ahead(a), ahead(b)) for a, b in v[p]])
            bwd = apply_link(link(lk_ref, 2, True, p), v[p])
            for cc in range(3):
                put_right(2, p, cc, fwd[cc][0] - behind(bwd[cc][0]),
                          fwd[cc][1] - behind(bwd[cc][1]))
        for cc in range(3):
            put_right(1, 2, cc,
                      -jnp.where(low, spill[0][1][cc][0], spill[1][0][cc][0]),
                      -jnp.where(low, spill[0][1][cc][1], spill[1][0][cc][1]))
        return 0

    lax.fori_loop(0, 24, group, 0)


    pl.semaphore_wait(barrier, 10)

    def product(b, depth):
        m, mu = b // 3, b % 3
        dims = (((1,), (1,)), ((), ()))

        def one(i):
            d = pl.ds(0, depth)
            lh, ll = left[m, i, 0, :, d], left[m, i, 1, :, d]
            rh, rl = right[mu, i, 0, :, d], right[mu, i, 1, :, d]
            dot = functools.partial(lax.dot_general, dimension_numbers=dims, preferred_element_type=F32)
            return (dot(lh, rh) + dot(lh, rl) + dot(ll, rh)).reshape(8, 2, 24, 384)

        k1 = one(0)
        e_ref[b, 1] = k1 + one(1)
        e_ref[b, 0] = k1 - one(2)

    def core_copy(b):
        return pltpu.make_async_remote_copy(
            src_ref=e_ref.at[b, :, :, 1 - c], dst_ref=cin.at[b], send_sem=csend.at[b],
            recv_sem=crecv.at[b], device_id=partner, device_id_type=MESH)

    def first(b, d, even):
        if even:
            src, to = cs.at[b, :, (y + d) % 4], on_y(d)
            dst = yin.at[b // 2, d - 1]
        else:
            xt = (x + d) % 4
            src, to = cs.at[b, xt % 2, :, xt // 2], on_x(d)
            dst = xin.at[b // 2, d - 1]
        return pltpu.make_async_remote_copy(
            src_ref=src, dst_ref=dst, send_sem=asend.at[b, d - 1],
            recv_sem=arecv.at[b, d - 1], device_id=to, device_id_type=MESH)

    def second(b, d, even):
        if even:
            xt = (x + d) % 4
            src, to = ys.at[b // 2, xt % 2, xt // 2], on_x(d)
        else:
            src, to = xs.at[b // 2, (y + d) % 4], on_y(d)
        return pltpu.make_async_remote_copy(
            src_ref=src, dst_ref=lin.at[b, d - 1], send_sem=bsend.at[b, d - 1],
            recv_sem=brecv.at[b, d - 1], device_id=to, device_id_type=MESH)

    def third(d):
        return pltpu.make_async_remote_copy(
            src_ref=zst.at[d], dst_ref=zin.at[d - 1], send_sem=zsend.at[d - 1],
            recv_sem=zrecv.at[d - 1], device_id=on_z(d), device_id_type=MESH)

    last = pltpu.make_async_remote_copy(
        src_ref=zs.at[0], dst_ref=zs.at[1], send_sem=lsend, recv_sem=lrecv,
        device_id=twin, device_id_type=MESH)

    def by_order(b, act):
        @pl.when(b % 2 == 0)
        def _():
            act(True)

        @pl.when(b % 2 == 1)
        def _():
            act(False)

    def over_core(b):
        core_copy(b).wait_recv()
        for i in range(8):
            for ri in range(2):
                cs[b, ri, i // 2, i % 2] = e_ref[b, ri, i, c] + cin[b, ri, i]

        def go(even):
            for d in (1, 2, 3):
                first(b, d, even).start()

        by_order(b, go)

    def over_first(b):
        h = b // 2

        def go(even):
            for d in (1, 2, 3):
                first(b, d, even).wait_recv()
            if even:
                for ri in range(2):
                    for g in range(2):
                        ys[h, ri, g] = (cs[b, ri, y, g] + yin[h, 0, ri, g]) + (
                            yin[h, 1, ri, g] + yin[h, 2, ri, g])
            else:
                for i in range(4):
                    xs[h, i] = (cs[b, xl, i, xh] + xin[h, 0, i]) + (xin[h, 1, i] + xin[h, 2, i])
            for d in (1, 2, 3):
                second(b, d, even).start()

        by_order(b, go)

    def over_second(b):
        def go(even):
            for d in (1, 2, 3):
                second(b, d, even).wait_recv()
            own = ys[b // 2, xl, xh] if even else xs[b // 2, y]
            t = (own + lin[b, 0]) + (lin[b, 1] + lin[b, 2])
            for d in range(4):
                zt = (z + d) % 4
                zst[d, b] = jnp.where(
                    lane_of((24, 128)) < 48,
                    pltpu.roll(t, (384 - 48 * zt) % 384, 1)[:, 0:128],
                    pltpu.roll(t, (624 - 48 * zt) % 384, 1)[:, 0:128])

        by_order(b, go)

    def turn(t, _):
        @pl.when(t < 6)
        def _():
            @pl.when(t % 3 == 1)
            def _():
                product(t, 1152)

            @pl.when(t % 3 != 1)
            def _():
                product(t, 768)

            core_copy(t).start()

        @pl.when(jnp.logical_and(t >= 1, t < 7))
        def _():
            over_core(t - 1)

        @pl.when(jnp.logical_and(t >= 3, t < 9))
        def _():
            over_first(t - 3)

        @pl.when(t >= 4)
        def _():
            over_second(t - 4)

        return 0

    lax.fori_loop(0, 10, turn, 0)

    for d in (1, 2, 3):
        third(d).start()
    for d in (1, 2, 3):
        third(d).wait_recv()
    zs[0] = (zst[0] + zin[0]) + (zin[1] + zin[2])
    last.start()
    last.wait_recv()
    for b in range(6):
        own = pltpu.roll(zs[0, b], (128 - 48 * xl) % 128, 1)[:, 0:48]
        other = pltpu.roll(zs[1, b], (128 - 48 * xl) % 128, 1)[:, 0:48]
        out_ref[b, xl] = own
        out_ref[b, 1 - xl] = other
    last.wait_send()
    for d in (1, 2, 3):
        third(d).wait_send()

    def sent(b, _):
        core_copy(b).wait_send()

        def go(even):
            for d in (1, 2, 3):
                first(b, d, even).wait_send()
                second(b, d, even).wait_send()

        by_order(b, go)
        return 0

    lax.fori_loop(0, 6, sent, 0)


def elementals(momenta, v, up, dn, lk, ulo):
    dma = pltpu.SemaphoreType.DMA
    return pl.pallas_call(
        elementals_kernel,
        out_shape=jax.ShapeDtypeStruct((6, 2, 24, 48), F32),
        in_specs=[pl.BlockSpec(memory_space=pltpu.SMEM)] + [VMEM] * 5,
        out_specs=VMEM,
        scratch_shapes=[
            pltpu.VMEM((2, 3, 2, 384, 1152), BF16),
            pltpu.VMEM((3, 3, 2, 384, 1152), BF16),
            pltpu.VMEM((2, 3, 2, 8, 128), F32),
            pltpu.VMEM((6, 2, 8, 2, 24, 384), F32),
            pltpu.VMEM((6, 2, 8, 24, 384), F32),
            pltpu.VMEM((6, 2, 4, 2, 24, 384), F32),
            pltpu.VMEM((3, 3, 2, 2, 24, 384), F32),
            pltpu.VMEM((3, 2, 2, 24, 384), F32),
            pltpu.VMEM((3, 3, 4, 24, 384), F32),
            pltpu.VMEM((3, 4, 24, 384), F32),
            pltpu.VMEM((4, 6, 24, 128), F32),
            pltpu.VMEM((3, 6, 24, 128), F32),
            pltpu.VMEM((2, 6, 24, 128), F32),
            pltpu.VMEM((6, 3, 24, 384), F32),
            dma((6,)), dma((6,)), dma((6, 3)), dma((6, 3)), dma((6, 3)), dma((6, 3)),
            dma((3,)), dma((3,)), dma(()), dma(()),
        ],
        compiler_params=pltpu.CompilerParams(
            collective_id=1, has_side_effects=True, vmem_limit_bytes=54 << 20),
        cost_estimate=pl.CostEstimate(flops=2 * 18 * 3 * 384 * 384 * 896, bytes_accessed=6 << 20, transcendentals=0),
        name="elementals",
    )(momenta, v, up, dn, lk, ulo)


def on_device(vectors, links, momenta, directions):
    out = elementals(momenta, *exchange(vectors, links)).reshape(2, 3, 2, 24, 48)
    picked = []
    for n in range(3):
        d = directions[n]
        picked.append(jnp.where(d == 0, out[:, 0], jnp.where(d == 1, out[:, 1], out[:, 2])))
    return jnp.stack(picked, axis=1)


def solution(mesh):
    placed = (
        P(None, None, "vec", "space", None),
        P(None, None, None, None, "space", None),
        P(),
        P(),
    )
    return jax.shard_map(
        on_device,
        mesh=mesh,
        in_specs=placed,
        out_specs=P(None, None, None, "space", "vec"),
        check_vma=False,
    )
```

time: 176 us -> 145 us (0.82)
  Pallas kernels: 162 us -> 130 us
    pallas_call x2 -> x1, Pallas kernels: 86.9 us -> 69.9 us  [elementals(): pl.pallas_call(elementals_kernel, out_shape=jax.ShapeDtypeStruct((6, 2, 2...]
    pallas_call x1, Pallas kernels: 74.9 us -> 60.1 us  [exchange(): pl.pallas_call(exchange_kernel, out_shape=[jax.ShapeDtypeStruct((2, 8, 43...]
where the time goes in v2:
time: 145 us; the launch traced here: 144 us
  Pallas kernels  130 us (90%)
  local copies, waits for them, and re-layouts  8.37 us (6%)
  between operations  3.73 us (3%)
  other arithmetic  1.55 us (1%)
    pallas_call x1, Pallas kernels, elementals(): pl.pallas_call(elementals_kernel, out_shape=jax.ShapeDtypeStruct((6, 2, 2...  69.9 us
    pallas_call x1, Pallas kernels, exchange(): pl.pallas_call(exchange_kernel, out_shape=[jax.ShapeDtypeStruct((2, 8, 43...  60.1 us
    unnamed x16, local copies, waits for them, and re-layouts  7.74 us

profile of v2, /device:TPU:0, one launch (start us, length us, event | category | flops | bytes accessed | tf_op | source)
XLA Modules:
  0.0 143.6 jit_solution(1916065580757183360)
XLA Ops:
  0.0 0.0 copy-start
  0.0 1.7 %copy-done = f32[2,3,48,1,2048]{4,3,2,1,0:T(1,128)S(1)} copy-done((f32[2,3,48,1,2048]{4,3,2,1,0:T(1,128)S(1)}, f32[2,3,48,1,2048]{4,3,2,1,0:T(1,128)}, u32[]{:S(2)}) %copy-start) | copy-done | bytes 2359320
  1.7 0.0 copy-start.1
  1.7 1.0 copy-done.1
  2.7 60.1 %exchange.1 = (f32[2,8,432,128]{3,2,1,0:T(8,128)S(1)}, f32[8,288,128]{2,1,0:T(8,128)S(1)}, f32[8,288,128]{2,1,0:T(8,128)S(1)}, f32[2,56,128]{2,1,0:T(8,128)S(1)}, f32[24,128]{1,0:T(8,128)S(1)}) custom-call(f32[4608,128]{1,0:T(8,128)S(1)} %bitcast.9, f32[864,128]{1,0:T(8,128)S(1)} %bitcast.10), custom_call_target="tpu_custom_call" | custom-call | tf_op jit(solution)/shard_map/exchange/pallas_call | solution.py:173
  62.8 0.0 copy-start.2
  62.8 1.7 %copy-done.2 = f32[2,8,432,128]{3,2,1,0:T(8,128)} copy-done((f32[2,8,432,128]{3,2,1,0:T(8,128)}, f32[2,8,432,128]{3,2,1,0:T(8,128)S(1)}, u32[]{:S(2)}) %copy-start.2) | copy-done | bytes 3538968
  64.6 0.0 copy-start.3
  64.6 1.0 copy-done.3
  65.6 0.0 copy-start.4
  65.6 1.1 copy-done.4
  66.7 0.0 copy-start.5
  66.7 0.6 copy-done.5
  67.3 0.0 copy-start.6
  67.3 0.6 copy-done.6
  67.9 0.0 copy-start.7
  67.9 69.9 %elementals.1 = f32[6,2,24,48]{3,2,1,0:T(8,128)} custom-call(s32[2,3]{1,0:T(2,128)} %mom_ref.1, f32[2,8,432,128]{3,2,1,0:T(8,128)} %copy-done.2, f32[8,288,128]{2,1,0:T(8,128)} %copy-done.3, f32[8,288,128]{2,1,0:T(8,128)} %copy-done.4, f32[2,56,128]{2,1,0:T(8,128)} %copy-done.5, f32[24,128]{1,0:T(8,128)} %copy-done.6), custom_call_target="tpu_custom_call" | custom-call | flops 14269022208 | bytes 6291456 | tf_op jit(solution)/shard_map/elementals/pallas_call | solution.py:522
  137.8 0.0 copy-done.7
  137.8 0.6 fusion
  142.1 0.9 select_select_fusion.2
  143.0 0.7 pad_maximum_fusion
Async XLA Ops:
  0.0 1.7 %copy-start = (f32[2,3,48,1,2048]{4,3,2,1,0:T(1,128)S(1)}, f32[2,3,48,1,2048]{4,3,2,1,0:T(1,128)}, u32[]{:S(2)}) copy-start(f32[2,3,48,1,2048]{4,3,2,1,0:T(1,128)} %param.4) | copy-start | bytes 7077892
  1.7 1.0 copy-start.1
  62.8 1.8 %copy-start.2 = (f32[2,8,432,128]{3,2,1,0:T(8,128)}, f32[2,8,432,128]{3,2,1,0:T(8,128)S(1)}, u32[]{:S(2)}) copy-start(f32[2,8,432,128]{3,2,1,0:T(8,128)S(1)} %get-tuple-element.10.v_ref) | copy-start | bytes 10616836
  64.6 1.0 copy-start.3
  65.6 1.1 copy-start.4
  66.7 0.6 copy-start.5
  67.3 0.6 copy-start.6
  67.9 69.9 %copy-start.7 = (s32[3]{0:T(128)S(1)}, s32[3]{0:T(128)}, u32[]{:S(2)}) copy-start(s32[3]{0:T(128)} %param.7) | copy-start | bytes 40

commit v3 on v2

v3 whole, which is shorter than its diff:
```python
import functools

import jax
import jax.numpy as jnp
from jax import lax
from jax.experimental import pallas as pl
from jax.experimental.pallas import tpu as pltpu
from jax.sharding import PartitionSpec as P

MESH = pl.DeviceIdType.MESH
F32 = jnp.float32
BF16 = jnp.bfloat16
VMEM = pl.BlockSpec(memory_space=pltpu.VMEM)
HBM = pl.BlockSpec(memory_space=pl.ANY)


def coords():
    s, k = lax.axis_index("space"), lax.axis_index("vec")
    return s // 4, (s // 2) % 2, s % 2, k // 4, k % 4


def lane_of(shape):
    return lax.broadcasted_iota(jnp.int32, shape, len(shape) - 1)


STEPS = ((2, 2), (1, 2), (3, 2), (2, 1), (2, 3), (1, 1), (3, 3), (1, 3),
         (3, 1), (2, 0), (0, 2), (0, 1), (0, 3), (1, 0), (3, 0), (0, 0))


def halves(t):
    hi = t.astype(BF16)
    return hi, (t - hi.astype(F32)).astype(BF16)


def apply_link(link, field):
    out = []
    for i in range(3):
        re = im = None
        for j in range(3):
            ur, ui = link(i, j)
            fr, fi = field[j]
            a = ur * fr - ui * fi
            b = ur * fi + ui * fr
            re = a if re is None else re + a
            im = b if im is None else im + b
        out.append((re, im))
    return out


def kernel(mom_ref, dir_ref, x_ref, u_ref, out_ref,
           stage, lstage, v_ref, up_ref, dn_ref, lk_ref, ulo_ref,
           left, right02, right1, tab, e_ref, cin, cs, yin, ys, xin, xs, zst, zin, zs, lin,
           send, recv, lsend, lrecv, fsend, frecv, usend, urecv,
           csend, crecv, asend, arecv, bsend, brecv, zsend, zrecv, tsend, trecv):
    y, xh, c, xl, z = coords()
    s, k = lax.axis_index("space"), lax.axis_index("vec")
    x = xh * 2 + xl
    selfish = c == xh

    def dev(y_, x_, c_, z_):
        return (y_ * 2 + x_ // 2) * 2 + c_, (x_ % 2) * 4 + z_

    def on_y(d):
        return dev((y + d) % 4, x, c, z)

    def on_x(d):
        return dev(y, (x + d) % 4, c, z)

    def on_z(d):
        return dev(y, x, c, (z + d) % 4)

    partner = dev(y, x, 1 - c, z)
    twin = dev(y, xh * 2 + 1 - xl, c, z)
    q = 2 * y + c
    qn, qp = (q + 1) % 8, (q + 7) % 8
    s_next = (qn // 2 * 2 + xh) * 2 + qn % 2
    s_prev = (qp // 2 * 2 + xh) * 2 + qp % 2

    def target(i):
        xt, zt = (x + STEPS[i][0]) % 4, (z + STEPS[i][1]) % 4
        return (y * 2 + xt // 2) * 2 + xh, (xt % 2) * 4 + zt, xt * 4 + zt

    def origin(i):
        return (y * 2 + c) * 2 + i % 2, i // 2

    barrier = pltpu.get_barrier_semaphore()

    def greet(i):
        st, kt, _j = target(i)

        @pl.when(jnp.logical_or(st != s, kt != k))
        def _():
            pl.semaphore_signal(barrier, inc=1, device_id=(st, kt), device_id_type=MESH)

        so, ko = origin(i)

        @pl.when(jnp.logical_or(so != s, ko != k))
        def _():
            pl.semaphore_signal(barrier, inc=1, device_id=(so, ko), device_id_type=MESH)

    for i in range(16):
        greet(i)
    pl.semaphore_signal(barrier, inc=1, device_id=(s_next, k), device_id_type=MESH)
    pl.semaphore_signal(barrier, inc=1, device_id=(s_prev, k), device_id_type=MESH)

    pl.semaphore_signal(barrier, inc=1, device_id=partner, device_id_type=MESH)
    for d in (1, 2, 3):
        for on in (on_y, on_x, on_z):
            pl.semaphore_signal(barrier, inc=1, device_id=on(d), device_id_type=MESH)

    for xt in range(2):
        j = (xt * 2 + xl) * 4 + z
        lstage[xt, 48:56, :] = jnp.zeros((8, 128), F32)
        lstage[xt, 0:54, :] = u_ref[pl.ds(j, 54, stride=16), :]
    pl.semaphore_wait(barrier, jnp.where(selfish, 42, 44))

    def link_copy(xt):
        return pltpu.make_async_remote_copy(
            src_ref=lstage.at[xt], dst_ref=lk_ref.at[c], send_sem=lsend.at[xt],
            recv_sem=lrecv.at[c], device_id=((y * 2 + xt) * 2 + xh, k), device_id_type=MESH)

    for xt in range(2):
        mine = jnp.logical_and(selfish, xh == xt)

        @pl.when(mine)
        def _():
            pltpu.make_async_copy(lstage.at[xt], lk_ref.at[c], lrecv.at[c]).start()

        @pl.when(jnp.logical_not(mine))
        def _():
            link_copy(xt).start()

    lane = lane_of((144, 128))

    def main_copy(i):
        st, kt, j = target(i)
        return pltpu.make_async_remote_copy(
            src_ref=stage.at[i], dst_ref=v_ref.at[c, k], send_sem=send.at[i],
            recv_sem=recv.at[c * 8 + k], device_id=(st, kt), device_id_type=MESH)

    def put(i):
        st, kt, j = target(i)
        nxt = (j + 1) % 16
        stage[i, 0:288, :] = x_ref[pl.ds(j, 288, stride=16), :]
        re = x_ref[pl.ds(nxt, 144, stride=16), :]
        im = x_ref[pl.ds(144 * 16 + nxt, 144, stride=16), :]
        stage[i, 288:432, :] = jnp.where(lane < 64, re, pltpu.roll(im, 64, 1))
        mine = jnp.logical_and(st == s, kt == k)

        @pl.when(mine)
        def _():
            pltpu.make_async_copy(stage.at[i], v_ref.at[c, k], recv.at[c * 8 + k]).start()

        @pl.when(jnp.logical_not(mine))
        def _():
            main_copy(i).start()

    for i in range(16):
        put(i)

    for p in range(2):
        pltpu.make_async_copy(lk_ref.at[p], lk_ref.at[p], lrecv.at[p]).wait()
    ulo = pltpu.make_async_remote_copy(
        src_ref=lk_ref.at[1, pl.ds(0, 24)], dst_ref=ulo_ref, send_sem=usend,
        recv_sem=urecv, device_id=(s_next, k), device_id_type=MESH)
    ulo.start()

    def hand(p, vb):
        return pltpu.make_async_remote_copy(
            src_ref=v_ref.at[p, vb, pl.ds(0, 288)],
            dst_ref=(up_ref if p == 0 else dn_ref).at[vb],
            send_sem=fsend.at[p, vb], recv_sem=frecv.at[p, vb],
            device_id=(s_prev if p == 0 else s_next, k), device_id_type=MESH)

    line = (xh * 2 + xl) * 4 + z
    lane1 = lane_of((8, 128))
    low1 = lane1 < 64
    for mm in range(2):
        for place in range(3):
            plane = 4 * y + 2 * c + (jnp.where(low1, 0, 1) if place == 2 else place)
            row = 2 * line + (2 if place == 2 else jnp.where(low1, 0, 1))
            col = lane1 & 63
            n = (((mom_ref[mm, 0] * plane) & 15) * 4 + ((mom_ref[mm, 1] * row) & 31) * 2
                 + ((mom_ref[mm, 2] * col) & 63)) & 63
            theta = n.astype(F32) * (2.0 * jnp.pi / 64)
            tab[mm, place, 0] = jnp.cos(theta)
            tab[mm, place, 1] = jnp.sin(theta)

    rows = 16
    lane = lane_of((rows, 128))
    low = lane < 64
    col = lane & 63

    def tools(vb, sub):
        at = pl.multiple_of(vb * 48 + sub * rows, rows)

        def comp(ref, reim, col_, *lead):
            first = pl.multiple_of(reim * 144 + col_ * 48 + sub * rows, rows)
            return ref[(*lead, vb, pl.ds(first, rows), slice(None))]

        def link(ref, mu_, dagger, *lead):
            def get(i, j):
                a, b = (j, i) if dagger else (i, j)
                r = mu_ * 18 + a * 3 + b
                ur = ref[(*lead, pl.ds(r, 1), slice(None))]
                ui = ref[(*lead, pl.ds(r + 9, 1), slice(None))]
                return ur, (-ui if dagger else ui)
            return get

        def put_right(mu_, place, cc, dr, di):
            kk = pl.ds((6 + cc if place == 2 else cc * 2 + place) * 128, 128)
            to = right1 if mu_ == 1 else right02
            off = pl.ds(pl.multiple_of(at + (384 if mu_ == 2 else 0), rows), rows)
            for i, t in enumerate((dr, di - dr, dr + di)):
                hi, lo = halves(t)
                to[i, 0, off, kk] = hi
                to[i, 1, off, kk] = lo

        return at, comp, link, put_right

    def inside(vb, sub):
        at, comp, link, put_right = tools(vb, sub)
        v = [[(comp(v_ref, 0, cc, p), comp(v_ref, 1, cc, p)) for cc in range(3)] for p in range(2)]
        packed = []
        for p in range(2):
            packed.append([
                v_ref[p, vb, pl.ds(pl.multiple_of(288 + cc * 48 + sub * rows, rows), rows), :]
                for cc in range(3)])
        ext = [
            (jnp.where(low, packed[0][cc], pltpu.roll(packed[1][cc], 64, 1)),
             jnp.where(low, pltpu.roll(packed[0][cc], 64, 1), packed[1][cc]))
            for cc in range(3)]

        for mm in range(2):
            for place in range(3):
                co, si = tab[mm, place, 0, 0:1], tab[mm, place, 1, 0:1]
                for cc in range(3):
                    vr, vi = ext[cc] if place == 2 else v[place][cc]
                    lr = vr * co - vi * si
                    li = -(vr * si + vi * co)
                    kk = pl.ds((6 + cc if place == 2 else cc * 2 + place) * 128, 128)
                    for i, t in enumerate((lr + li, lr, li)):
                        hi, lo = halves(t)
                        left[mm, i, 0, pl.ds(at, rows), kk] = hi
                        left[mm, i, 1, pl.ds(at, rows), kk] = lo

        spill = []
        for p in range(2):
            shifted = []
            for cc in range(3):
                vr, vi = v[p][cc]
                shifted.append((
                    pltpu.roll(jnp.where(low, packed[p][cc], vr), 64, 1),
                    jnp.where(low, pltpu.roll(vi, 64, 1), packed[p][cc])))
            fwd = apply_link(link(lk_ref, 1, False, p), shifted)
            bwd = apply_link(link(lk_ref, 1, True, p), v[p])
            turned = []
            for cc in range(3):
                tr, ti = pltpu.roll(bwd[cc][0], 64, 1), pltpu.roll(bwd[cc][1], 64, 1)
                turned.append((tr, ti))
                put_right(1, p, cc, fwd[cc][0] - jnp.where(low, 0.0, tr),
                          fwd[cc][1] - jnp.where(low, 0.0, ti))
            spill.append((bwd, turned))
            def ahead(t):
                return jnp.where(col == 63, pltpu.roll(t, 63, 1), pltpu.roll(t, 127, 1))

            def behind(t):
                return jnp.where(col == 0, pltpu.roll(t, 65, 1), pltpu.roll(t, 1, 1))

            fwd = apply_link(link(lk_ref, 2, False, p), [(ahead(a), ahead(b)) for a, b in v[p]])
            bwd = apply_link(link(lk_ref, 2, True, p), v[p])
            for cc in range(3):
                put_right(2, p, cc, fwd[cc][0] - behind(bwd[cc][0]),
                          fwd[cc][1] - behind(bwd[cc][1]))
        for cc in range(3):
            put_right(1, 2, cc,
                      -jnp.where(low, spill[0][1][cc][0], spill[1][0][cc][0]),
                      -jnp.where(low, spill[0][1][cc][1], spill[1][0][cc][1]))

    def across(vb, sub):
        at, comp, link, put_right = tools(vb, sub)
        v = [[(comp(v_ref, 0, cc, p), comp(v_ref, 1, cc, p)) for cc in range(3)] for p in range(2)]
        above = [(comp(up_ref, 0, cc), comp(up_ref, 1, cc)) for cc in range(3)]
        below = [(comp(dn_ref, 0, cc), comp(dn_ref, 1, cc)) for cc in range(3)]
        for p in range(2):
            fwd = apply_link(link(lk_ref, 0, False, p), v[1] if p == 0 else above)
            bwd = (apply_link(link(ulo_ref, 0, True), below) if p == 0
                   else apply_link(link(lk_ref, 0, True, 0), v[0]))
            for cc in range(3):
                put_right(0, p, cc, fwd[cc][0] - bwd[cc][0], fwd[cc][1] - bwd[cc][1])

    def arrivals(other):
        number = 0
        for far in range(2):
            for low_ in range(2):
                digits = [
                    xs_ * 4 + dz for dx, dz in STEPS for xs_ in range(2)
                    if (2 * far + low_ - xs_) % 4 == dx]
                value = sum(t * 8 ** n for n, t in enumerate(digits))
                hit = jnp.logical_and((xh != c) == ((far == 1) != other), xl == low_)
                number = jnp.where(hit, value, number)
        return number

    def vector_block(number):
        digit = number % 8
        return digit // 4 * 4 + (z + 4 - digit % 4) % 4

    def take(t, number):
        vb = vector_block(number)
        for p in range(2):
            pltpu.make_async_copy(v_ref.at[p, vb], v_ref.at[p, vb], recv.at[p * 8 + vb]).wait()
            hand(p, vb).start()

        def sub_loop(sub, _):
            inside(vb, sub)
            return 0

        lax.fori_loop(0, 3, sub_loop, 0)
        return number // 8

    lax.fori_loop(0, 8, take, arrivals(False))
    ulo.wait_recv()

    def join(t, number):
        vb = vector_block(number)
        for p in range(2):
            hand(p, vb).wait_recv()

        def sub_loop(sub, _):
            across(vb, sub)
            return 0

        lax.fori_loop(0, 3, sub_loop, 0)
        return number // 8

    lax.fori_loop(0, 8, join, arrivals(True))

    dims = (((1,), (1,)), ((), ()))
    dot = functools.partial(lax.dot_general, dimension_numbers=dims, preferred_element_type=F32)

    def product_pair(m):
        def one(i):
            d = pl.ds(0, 768)
            lh, ll = left[m, i, 0, :, d], left[m, i, 1, :, d]
            rh, rl = right02[i, 0], right02[i, 1]
            return dot(lh, rh) + dot(lh, rl) + dot(ll, rh)

        def keep(ri, t):
            e_ref[3 * m, ri] = t[:, 0:384].reshape(8, 2, 24, 384)
            e_ref[3 * m + 1, ri] = t[:, 384:768].reshape(8, 2, 24, 384)

        k1 = one(0)
        keep(0, k1 - one(2))
        keep(1, k1 + one(1))

    def product_one(m):
        def one(i):
            lh, ll = left[m, i, 0], left[m, i, 1]
            rh, rl = right1[i, 0], right1[i, 1]
            return (dot(lh, rh) + dot(lh, rl) + dot(ll, rh)).reshape(8, 2, 24, 384)

        k1 = one(0)
        e_ref[3 * m + 2, 0] = k1 - one(2)
        e_ref[3 * m + 2, 1] = k1 + one(1)

    def core_copy(b):
        return pltpu.make_async_remote_copy(
            src_ref=e_ref.at[b, :, :, 1 - c], dst_ref=cin.at[b], send_sem=csend.at[b],
            recv_sem=crecv.at[b], device_id=partner, device_id_type=MESH)

    def first(b, d, even):
        if even:
            src, to = cs.at[b, :, (y + d) % 4], on_y(d)
            dst = yin.at[b // 2, d - 1]
        else:
            xt = (x + d) % 4
            src, to = cs.at[b, xt % 2, :, xt // 2], on_x(d)
            dst = xin.at[b // 2, d - 1]
        return pltpu.make_async_remote_copy(
            src_ref=src, dst_ref=dst, send_sem=asend.at[b, d - 1],
            recv_sem=arecv.at[b, d - 1], device_id=to, device_id_type=MESH)

    def second(b, d, even):
        if even:
            xt = (x + d) % 4
            src, to = ys.at[b // 2, xt % 2, xt // 2], on_x(d)
        else:
            src, to = xs.at[b // 2, (y + d) % 4], on_y(d)
        return pltpu.make_async_remote_copy(
            src_ref=src, dst_ref=lin.at[b, d - 1], send_sem=bsend.at[b, d - 1],
            recv_sem=brecv.at[b, d - 1], device_id=to, device_id_type=MESH)

    def third(d):
        return pltpu.make_async_remote_copy(
            src_ref=zst.at[d], dst_ref=zin.at[d - 1], send_sem=zsend.at[d - 1],
            recv_sem=zrecv.at[d - 1], device_id=on_z(d), device_id_type=MESH)

    last = pltpu.make_async_remote_copy(
        src_ref=zs.at[0], dst_ref=zs.at[1], send_sem=tsend, recv_sem=trecv,
        device_id=twin, device_id_type=MESH)

    def by_order(b, act):
        if isinstance(b, int):
            act(b % 2 == 0)
            return

        @pl.when(b % 2 == 0)
        def _():
            act(True)

        @pl.when(b % 2 == 1)
        def _():
            act(False)

    def over_core(b):
        core_copy(b).wait_recv()
        for i in range(8):
            for ri in range(2):
                cs[b, ri, i // 2, i % 2] = e_ref[b, ri, i, c] + cin[b, ri, i]

        def go(even):
            for d in (1, 2, 3):
                first(b, d, even).start()

        by_order(b, go)

    def over_first(b):
        h = b // 2

        def go(even):
            for d in (1, 2, 3):
                first(b, d, even).wait_recv()
            if even:
                for ri in range(2):
                    for g in range(2):
                        ys[h, ri, g] = (cs[b, ri, y, g] + yin[h, 0, ri, g]) + (
                            yin[h, 1, ri, g] + yin[h, 2, ri, g])
            else:
                for i in range(4):
                    xs[h, i] = (cs[b, xl, i, xh] + xin[h, 0, i]) + (xin[h, 1, i] + xin[h, 2, i])
            for d in (1, 2, 3):
                second(b, d, even).start()

        by_order(b, go)

    def over_second(b):
        def go(even):
            for d in (1, 2, 3):
                second(b, d, even).wait_recv()
            own = ys[b // 2, xl, xh] if even else xs[b // 2, y]
            t = (own + lin[b, 0]) + (lin[b, 1] + lin[b, 2])
            for d in range(4):
                zt = (z + d) % 4
                zst[d, b] = jnp.where(
                    lane_of((24, 128)) < 48,
                    pltpu.roll(t, (384 - 48 * zt) % 384, 1)[:, 0:128],
                    pltpu.roll(t, (624 - 48 * zt) % 384, 1)[:, 0:128])

        by_order(b, go)

    def turn(m, _):
        product_pair(m)
        core_copy(3 * m).start()
        core_copy(3 * m + 1).start()

        @pl.when(m == 1)
        def _():
            over_core(2)
            over_first(0)

        product_one(m)
        core_copy(3 * m + 2).start()
        over_core(3 * m)
        over_core(3 * m + 1)
        return 0

    lax.fori_loop(0, 2, turn, 0)
    over_core(5)
    over_first(1)
    over_first(2)
    over_second(0)
    over_second(1)
    over_first(3)
    over_second(2)
    over_first(4)
    over_second(3)
    over_first(5)
    over_second(4)
    over_second(5)

    for d in (1, 2, 3):
        third(d).start()
    for d in (1, 2, 3):
        third(d).wait_recv()
    zs[0] = (zst[0] + zin[0]) + (zin[1] + zin[2])
    last.start()
    last.wait_recv()
    def mine(which, b):
        return pltpu.roll(zs[which, b], (128 - 48 * xl) % 128, 1)[:, 0:48]

    for m in range(2):
        for which in range(2):
            d0, d2, d1 = (mine(which, 3 * m + i) for i in range(3))
            for n in range(3):
                d = dir_ref[n]
                out_ref[m, n, xl if which == 0 else 1 - xl] = jnp.where(
                    d == 0, d0, jnp.where(d == 1, d1, d2))
    last.wait_send()
    for d in (1, 2, 3):
        third(d).wait_send()

    def gone(b, _):
        core_copy(b).wait_send()

        def go(even):
            for d in (1, 2, 3):
                first(b, d, even).wait_send()
                second(b, d, even).wait_send()

        by_order(b, go)
        return 0

    lax.fori_loop(0, 6, gone, 0)

    def finish(i, _):
        for p in range(2):
            hand(p, i).wait_send()
        return 0

    lax.fori_loop(0, 8, finish, 0)
    ulo.wait_send()
    for xt in range(2):

        @pl.when(jnp.logical_not(jnp.logical_and(selfish, xh == xt)))
        def _():
            link_copy(xt).wait_send()

    def sent(i):
        st, kt, _j = target(i)

        @pl.when(jnp.logical_or(st != s, kt != k))
        def _():
            main_copy(i).wait_send()

    for i in range(16):
        sent(i)


def elementals(vectors, links, momenta, directions):
    dma = pltpu.SemaphoreType.DMA
    smem = pl.BlockSpec(memory_space=pltpu.SMEM)
    return pl.pallas_call(
        kernel,
        out_shape=jax.ShapeDtypeStruct((2, 3, 2, 24, 48), F32),
        in_specs=[smem, smem, VMEM, VMEM],
        out_specs=VMEM,
        scratch_shapes=[
            pltpu.VMEM((16, 432, 128), F32),
            pltpu.VMEM((2, 56, 128), F32),
            pltpu.VMEM((2, 8, 432, 128), F32),
            pltpu.VMEM((8, 288, 128), F32),
            pltpu.VMEM((8, 288, 128), F32),
            pltpu.VMEM((2, 56, 128), F32),
            pltpu.VMEM((24, 128), F32),
            pltpu.VMEM((2, 3, 2, 384, 1152), BF16),
            pltpu.VMEM((3, 2, 768, 768), BF16),
            pltpu.VMEM((3, 2, 384, 1152), BF16),
            pltpu.VMEM((2, 3, 2, 8, 128), F32),
            pltpu.VMEM((6, 2, 8, 2, 24, 384), F32),
            pltpu.VMEM((6, 2, 8, 24, 384), F32),
            pltpu.VMEM((6, 2, 4, 2, 24, 384), F32),
            pltpu.VMEM((3, 3, 2, 2, 24, 384), F32),
            pltpu.VMEM((3, 2, 2, 24, 384), F32),
            pltpu.VMEM((3, 3, 4, 24, 384), F32),
            pltpu.VMEM((3, 4, 24, 384), F32),
            pltpu.VMEM((4, 6, 24, 128), F32),
            pltpu.VMEM((3, 6, 24, 128), F32),
            pltpu.VMEM((2, 6, 24, 128), F32),
            pltpu.VMEM((6, 3, 24, 384), F32),
            dma((16,)), dma((16,)), dma((2,)), dma((2,)),
            dma((2, 8)), dma((2, 8)), dma(()), dma(()),
            dma((6,)), dma((6,)), dma((6, 3)), dma((6, 3)), dma((6, 3)), dma((6, 3)),
            dma((3,)), dma((3,)), dma(()), dma(()),
        ],
        compiler_params=pltpu.CompilerParams(
            collective_id=0, has_side_effects=True, vmem_limit_bytes=60 << 20),
        cost_estimate=pl.CostEstimate(flops=2 * 18 * 3 * 384 * 384 * 896, bytes_accessed=6 << 20, transcendentals=0),
        name="elementals",
    )(momenta, directions, vectors.reshape(288 * 16, 128), links.reshape(54 * 16, 128))


def solution(mesh):
    placed = (
        P(None, None, "vec", "space", None),
        P(None, None, None, None, "space", None),
        P(),
        P(),
    )
    return jax.shard_map(
        elementals,
        mesh=mesh,
        in_specs=placed,
        out_specs=P(None, None, None, "space", "vec"),
        check_vma=False,
    )
```

time: 145 us -> 124 us (0.86); the launches traced: 144 us -> 124 us
  Pallas kernels: 130 us -> 123 us
  local copies, waits for them, and re-layouts: 8.37 us -> 1.58 us
  between operations: 3.73 us -> 0.01 us
  other arithmetic: 1.55 us -> 0 us
    pallas_call x2 -> x1, Pallas kernels: 130 us -> 123 us  [elementals(): pl.pallas_call(kernel, out_shape=jax.ShapeDtypeStruct((2, 3, 2, 24, 48),...]
    unnamed x16 -> x1, local copies, waits for them, and re-layouts: 7.74 us -> 1.58 us
where the time goes in v3:
time: 124 us
  Pallas kernels  123 us (99%)
  local copies, waits for them, and re-layouts  1.58 us (1%)
    pallas_call x1, Pallas kernels, elementals(): pl.pallas_call(kernel, out_shape=jax.ShapeDtypeStruct((2, 3, 2, 24, 48),...  123 us

profile of v3, /device:TPU:0, one launch (start us, length us, event | category | flops | bytes accessed | tf_op | source)
XLA Modules:
  0.0 124.1 jit_solution(2949994246464932361)
XLA Ops:
  0.0 122.5 %elementals.1 = f32[2,3,2,24,48]{4,3,2,1,0:T(8,128)} custom-call(s32[2,3]{1,0:T(2,128)} %mom_ref.1, s32[3]{0:T(128)} %dir_ref.1, f32[4608,128]{1,0:T(8,128)} %bitcast.2, f32[864,128]{1,0:T(8,128)} %bitcast.3), custom_call_target="tpu_custom_call" | custom-call | flops 14269022208 | bytes 6291456 | tf_op jit(solution)/shard_map/elementals/pallas_call | solution.py:552
  122.5 1.6 %copy.6 = f32[2,3,2,24,48]{4,3,2,1,0:T(8,128)} copy(f32[2,3,2,24,48]{4,3,2,1,0:T(8,128)} %elementals.1) | data formatting | bytes 110592

commit v4 on v3

--- a/solution.py
+++ b/solution.py
@@ -49,9 +49,9 @@
 
 def kernel(mom_ref, dir_ref, x_ref, u_ref, out_ref,
            stage, lstage, v_ref, up_ref, dn_ref, lk_ref, ulo_ref,
-           left, right02, right1, tab, e_ref, cin, cs, yin, ys, xin, xs, zst, zin, zs, lin,
+           left, right02, right1, tab, e_ref, cin, cs, yin, ys, xin, xs, zst, zin, lin,
            send, recv, lsend, lrecv, fsend, frecv, usend, urecv,
-           csend, crecv, asend, arecv, bsend, brecv, zsend, zrecv, tsend, trecv):
+           csend, crecv, asend, arecv, bsend, brecv, zsend, zrecv):
     y, xh, c, xl, z = coords()
     s, k = lax.axis_index("space"), lax.axis_index("vec")
     x = xh * 2 + xl
@@ -70,7 +70,7 @@
         return dev(y, x, c, (z + d) % 4)
 
     partner = dev(y, x, 1 - c, z)
-    twin = dev(y, xh * 2 + 1 - xl, c, z)
+    s_turned = (z * 2 + xh) * 2 + c
     q = 2 * y + c
     qn, qp = (q + 1) % 8, (q + 7) % 8
     s_next = (qn // 2 * 2 + xh) * 2 + qn % 2
@@ -105,14 +105,29 @@
 
     pl.semaphore_signal(barrier, inc=1, device_id=partner, device_id_type=MESH)
     for d in (1, 2, 3):
-        for on in (on_y, on_x, on_z):
+        for on in (on_y, on_x):
             pl.semaphore_signal(barrier, inc=1, device_id=on(d), device_id_type=MESH)
+    for kt in range(8):
+
+        @pl.when(kt != k)
+        def _():
+            pl.semaphore_signal(barrier, inc=1, device_id=(s, kt), device_id_type=MESH)
+
+        @pl.when(jnp.logical_or(s_turned != s, kt != k))
+        def _():
+            pl.semaphore_signal(barrier, inc=1, device_id=(s_turned, kt), device_id_type=MESH)
+
+        so, ko = (kt % 4 * 2 + xh) * 2 + c, kt // 4 * 4 + y
+
+        @pl.when(jnp.logical_or(so != s, ko != k))
+        def _():
+            pl.semaphore_signal(barrier, inc=1, device_id=(so, ko), device_id_type=MESH)
 
     for xt in range(2):
         j = (xt * 2 + xl) * 4 + z
         lstage[xt, 48:56, :] = jnp.zeros((8, 128), F32)
         lstage[xt, 0:54, :] = u_ref[pl.ds(j, 54, stride=16), :]
-    pl.semaphore_wait(barrier, jnp.where(selfish, 42, 44))
+    pl.semaphore_wait(barrier, jnp.where(selfish, 62, 64) - jnp.where(y == z, 2, 0))
 
     def link_copy(xt):
         return pltpu.make_async_remote_copy(
@@ -319,7 +334,6 @@
         return number // 8
 
     lax.fori_loop(0, 8, take, arrivals(False))
-    ulo.wait_recv()
 
     def join(t, number):
         vb = vector_block(number)
@@ -333,194 +347,214 @@
         lax.fori_loop(0, 3, sub_loop, 0)
         return number // 8
 
-    lax.fori_loop(0, 8, join, arrivals(True))
-
     dims = (((1,), (1,)), ((), ()))
     dot = functools.partial(lax.dot_general, dimension_numbers=dims, preferred_element_type=F32)
 
-    def product_pair(m):
-        def one(i):
-            d = pl.ds(0, 768)
-            lh, ll = left[m, i, 0, :, d], left[m, i, 1, :, d]
-            rh, rl = right02[i, 0], right02[i, 1]
-            return dot(lh, rh) + dot(lh, rl) + dot(ll, rh)
-
-        def keep(ri, t):
-            e_ref[3 * m, ri] = t[:, 0:384].reshape(8, 2, 24, 384)
-            e_ref[3 * m + 1, ri] = t[:, 384:768].reshape(8, 2, 24, 384)
-
-        k1 = one(0)
-        keep(0, k1 - one(2))
-        keep(1, k1 + one(1))
-
-    def product_one(m):
-        def one(i):
-            lh, ll = left[m, i, 0], left[m, i, 1]
-            rh, rl = right1[i, 0], right1[i, 1]
-            return (dot(lh, rh) + dot(lh, rl) + dot(ll, rh)).reshape(8, 2, 24, 384)
-
-        k1 = one(0)
-        e_ref[3 * m + 2, 0] = k1 - one(2)
-        e_ref[3 * m + 2, 1] = k1 + one(1)
-
-    def core_copy(b):
-        return pltpu.make_async_remote_copy(
-            src_ref=e_ref.at[b, :, :, 1 - c], dst_ref=cin.at[b], send_sem=csend.at[b],
-            recv_sem=crecv.at[b], device_id=partner, device_id_type=MESH)
-
-    def first(b, d, even):
-        if even:
-            src, to = cs.at[b, :, (y + d) % 4], on_y(d)
-            dst = yin.at[b // 2, d - 1]
+    def one(m, i):
+        lh, ll = left[m, i, 0], left[m, i, 1]
+        rh, rl = right1[i, 0], right1[i, 1]
+        return (dot(lh, rh) + dot(lh, rl) + dot(ll, rh)).reshape(8, 2, 24, 384)
+
+    def one_real(m):
+        k1 = one(m, 0)
+        e_ref[m, 1] = k1
+        e_ref[m, 0] = k1 - one(m, 2)
+        core_copy(m, 0).start()
+
+    def one_imag(m):
+        e_ref[m, 1] += one(m, 1)
+        core_copy(m, 1).start()
+
+    def pair(m, i):
+        d = pl.ds(0, 768)
+        lh, ll = left[m, i, 0, :, d], left[m, i, 1, :, d]
+        rh, rl = right02[i, 0], right02[i, 1]
+        t = dot(lh, rh) + dot(lh, rl) + dot(ll, rh)
+        return t[:, 0:384].reshape(8, 2, 24, 384), t[:, 384:768].reshape(8, 2, 24, 384)
+
+    def pair_real(m):
+        b = 2 + 2 * m
+        for n, t in enumerate(pair(m, 0)):
+            e_ref[b + n, 1] = t
+        for n, t in enumerate(pair(m, 2)):
+            e_ref[b + n, 0] = e_ref[b + n, 1] - t
+            core_copy(b + n, 0).start()
+
+    def pair_imag(m):
+        b = 2 + 2 * m
+        for n, t in enumerate(pair(m, 1)):
+            e_ref[b + n, 1] += t
+            core_copy(b + n, 1).start()
+
+    def core_copy(b, ri):
+        return pltpu.make_async_remote_copy(
+            src_ref=e_ref.at[b, ri, :, 1 - c], dst_ref=cin.at[b, ri], send_sem=csend.at[b, ri],
+            recv_sem=crecv.at[b, ri], device_id=partner, device_id_type=MESH)
+
+    slot = {0: 0, 1: 1, 2: 2, 4: 3, 3: 0, 5: 1}
+
+    def rows_first(b, d, ri):
+        at, to = (z, on_z) if b < 2 else (y, on_y)
+        return pltpu.make_async_remote_copy(
+            src_ref=cs.at[b, ri, (at + d) % 4], dst_ref=yin.at[slot[b], d - 1, ri],
+            send_sem=asend.at[b, 3 * ri + d - 1], recv_sem=arecv.at[b, 3 * ri + d - 1],
+            device_id=to(d), device_id_type=MESH)
+
+    def x_first(b, d):
+        xt = (x + d) % 4
+        return pltpu.make_async_remote_copy(
+            src_ref=cs.at[b, xt % 2, :, xt // 2], dst_ref=xin.at[slot[b], d - 1],
+            send_sem=asend.at[b, d - 1], recv_sem=arecv.at[b, d - 1],
+            device_id=on_x(d), device_id_type=MESH)
+
+    def by_rows(b):
+        return b not in (3, 5)
+
+    def second(b, d):
+        if by_rows(b):
+            xt = (x + d) % 4
+            src, to = ys.at[slot[b], xt % 2, xt // 2], on_x(d)
         else:
-            xt = (x + d) % 4
-            src, to = cs.at[b, xt % 2, :, xt // 2], on_x(d)
-            dst = xin.at[b // 2, d - 1]
-        return pltpu.make_async_remote_copy(
-            src_ref=src, dst_ref=dst, send_sem=asend.at[b, d - 1],
-            recv_sem=arecv.at[b, d - 1], device_id=to, device_id_type=MESH)
-
-    def second(b, d, even):
-        if even:
-            xt = (x + d) % 4
-            src, to = ys.at[b // 2, xt % 2, xt // 2], on_x(d)
-        else:
-            src, to = xs.at[b // 2, (y + d) % 4], on_y(d)
+            src, to = xs.at[slot[b], (y + d) % 4], on_y(d)
         return pltpu.make_async_remote_copy(
             src_ref=src, dst_ref=lin.at[b, d - 1], send_sem=bsend.at[b, d - 1],
             recv_sem=brecv.at[b, d - 1], device_id=to, device_id_type=MESH)
 
-    def third(d):
-        return pltpu.make_async_remote_copy(
-            src_ref=zst.at[d], dst_ref=zin.at[d - 1], send_sem=zsend.at[d - 1],
-            recv_sem=zrecv.at[d - 1], device_id=on_z(d), device_id_type=MESH)
-
-    last = pltpu.make_async_remote_copy(
-        src_ref=zs.at[0], dst_ref=zs.at[1], send_sem=tsend, recv_sem=trecv,
-        device_id=twin, device_id_type=MESH)
-
-    def by_order(b, act):
-        if isinstance(b, int):
-            act(b % 2 == 0)
-            return
-
-        @pl.when(b % 2 == 0)
-        def _():
-            act(True)
-
-        @pl.when(b % 2 == 1)
-        def _():
-            act(False)
-
-    def over_core(b):
-        core_copy(b).wait_recv()
+    def third(n, kt):
+        at = xl * 4 + y if n == 0 else k
+        return pltpu.make_async_remote_copy(
+            src_ref=zst.at[n, kt], dst_ref=zin.at[n, at], send_sem=zsend.at[n, kt],
+            recv_sem=zrecv.at[n, at], device_id=(s_turned if n == 0 else s, kt), device_id_type=MESH)
+
+    def away(n, kt):
+        return jnp.logical_or(y != z, kt != k) if n == 0 else kt != k
+
+    def over_core(b, ri):
+        core_copy(b, ri).wait_recv()
         for i in range(8):
+            cs[b, ri, i // 2, i % 2] = e_ref[b, ri, i, c] + cin[b, ri, i]
+        for d in (1, 2, 3):
+            if by_rows(b):
+                rows_first(b, d, ri).start()
+            else:
+
+                @pl.when((x + d) % 2 == ri)
+                def _():
+                    x_first(b, d).start()
+
+    def over_first(b):
+        n = slot[b]
+        if by_rows(b):
+            q = z if b < 2 else y
             for ri in range(2):
-                cs[b, ri, i // 2, i % 2] = e_ref[b, ri, i, c] + cin[b, ri, i]
-
-        def go(even):
+                for d in (1, 2, 3):
+                    rows_first(b, d, ri).wait_recv()
+                for g in range(2):
+                    ys[n, ri, g] = (cs[b, ri, q, g] + yin[n, 0, ri, g]) + (
+                        yin[n, 1, ri, g] + yin[n, 2, ri, g])
+        else:
             for d in (1, 2, 3):
-                first(b, d, even).start()
-
-        by_order(b, go)
-
-    def over_first(b):
-        h = b // 2
-
-        def go(even):
+                x_first(b, d).wait_recv()
+            for i in range(4):
+                xs[n, i] = (cs[b, xl, i, xh] + xin[n, 0, i]) + (xin[n, 1, i] + xin[n, 2, i])
+        for d in (1, 2, 3):
+            second(b, d).start()
+
+    def over_second(n):
+        sums = []
+        for b in (2 * n, 2 * n + 1):
             for d in (1, 2, 3):
-                first(b, d, even).wait_recv()
-            if even:
-                for ri in range(2):
-                    for g in range(2):
-                        ys[h, ri, g] = (cs[b, ri, y, g] + yin[h, 0, ri, g]) + (
-                            yin[h, 1, ri, g] + yin[h, 2, ri, g])
-            else:
-                for i in range(4):
-                    xs[h, i] = (cs[b, xl, i, xh] + xin[h, 0, i]) + (xin[h, 1, i] + xin[h, 2, i])
-            for d in (1, 2, 3):
-                second(b, d, even).start()
-
-        by_order(b, go)
-
-    def over_second(b):
-        def go(even):
-            for d in (1, 2, 3):
-                second(b, d, even).wait_recv()
-            own = ys[b // 2, xl, xh] if even else xs[b // 2, y]
-            t = (own + lin[b, 0]) + (lin[b, 1] + lin[b, 2])
-            for d in range(4):
-                zt = (z + d) % 4
-                zst[d, b] = jnp.where(
-                    lane_of((24, 128)) < 48,
-                    pltpu.roll(t, (384 - 48 * zt) % 384, 1)[:, 0:128],
-                    pltpu.roll(t, (624 - 48 * zt) % 384, 1)[:, 0:128])
-
-        by_order(b, go)
-
-    def turn(m, _):
-        product_pair(m)
-        core_copy(3 * m).start()
-        core_copy(3 * m + 1).start()
-
-        @pl.when(m == 1)
-        def _():
-            over_core(2)
-            over_first(0)
-
-        product_one(m)
-        core_copy(3 * m + 2).start()
-        over_core(3 * m)
-        over_core(3 * m + 1)
-        return 0
-
-    lax.fori_loop(0, 2, turn, 0)
-    over_core(5)
+                second(b, d).wait_recv()
+            own = ys[slot[b], xl, xh] if by_rows(b) else xs[slot[b], y]
+            sums.append((own + lin[b, 0]) + (lin[b, 1] + lin[b, 2]))
+        first_half = lane_of((24, 128)) < 64
+        for kt in range(8):
+            zst[n, kt] = jnp.where(
+                first_half,
+                pltpu.roll(sums[0], (384 - 48 * kt) % 384, 1)[:, 0:128],
+                pltpu.roll(sums[1], (448 - 48 * kt) % 384, 1)[:, 0:128])
+
+            @pl.when(away(n, kt))
+            def _():
+                third(n, kt).start()
+
+        if n == 0:
+
+            @pl.when(y == z)
+            def _():
+                zin[n, k] = zst[n, k]
+        else:
+            zin[n, k] = zst[n, k]
+
+    one_real(0)
+    one_imag(0)
+    over_core(0, 0)
+    ulo.wait_recv()
+    lax.fori_loop(0, 8, join, arrivals(True))
+    over_core(0, 1)
+    pair_real(0)
+    pair_imag(0)
+    over_core(2, 0)
+    over_core(3, 0)
+    pair_real(1)
+    over_core(2, 1)
+    over_core(3, 1)
+    over_first(0)
+    pair_imag(1)
+    over_core(4, 0)
+    over_core(5, 0)
+    one_real(1)
+    over_core(4, 1)
+    over_core(5, 1)
+    one_imag(1)
+    over_core(1, 0)
+    over_first(2)
+    over_first(3)
+    over_core(1, 1)
+    over_first(4)
+    over_first(5)
+    over_second(1)
     over_first(1)
-    over_first(2)
+    over_second(2)
     over_second(0)
-    over_second(1)
-    over_first(3)
-    over_second(2)
-    over_first(4)
-    over_second(3)
-    over_first(5)
-    over_second(4)
-    over_second(5)
-
-    for d in (1, 2, 3):
-        third(d).start()
-    for d in (1, 2, 3):
-        third(d).wait_recv()
-    zs[0] = (zst[0] + zin[0]) + (zin[1] + zin[2])
-    last.start()
-    last.wait_recv()
-    def mine(which, b):
-        return pltpu.roll(zs[which, b], (128 - 48 * xl) % 128, 1)[:, 0:48]
-
+
+    def arrive(n):
+        for kt in range(8):
+
+            @pl.when(away(n, kt))
+            def _():
+                pltpu.make_async_copy(zin.at[n, kt], zin.at[n, kt], zrecv.at[n, kt]).wait()
+
+    for n in range(3):
+        arrive(n)
+    done = {}
+    for n in range(3):
+        for ri in range(2):
+            t = (zin[n, 4 * ri] + zin[n, 4 * ri + 1]) + (zin[n, 4 * ri + 2] + zin[n, 4 * ri + 3])
+            done[2 * n, ri] = t[:, 0:48]
+            done[2 * n + 1, ri] = pltpu.roll(t, 64, 1)[:, 0:48]
     for m in range(2):
-        for which in range(2):
-            d0, d2, d1 = (mine(which, 3 * m + i) for i in range(3))
+        for ri in range(2):
+            d0, d1, d2 = done[2 + 2 * m, ri], done[m, ri], done[3 + 2 * m, ri]
             for n in range(3):
                 d = dir_ref[n]
-                out_ref[m, n, xl if which == 0 else 1 - xl] = jnp.where(
-                    d == 0, d0, jnp.where(d == 1, d1, d2))
-    last.wait_send()
-    for d in (1, 2, 3):
-        third(d).wait_send()
-
-    def gone(b, _):
-        core_copy(b).wait_send()
-
-        def go(even):
-            for d in (1, 2, 3):
-                first(b, d, even).wait_send()
-                second(b, d, even).wait_send()
-
-        by_order(b, go)
-        return 0
-
-    lax.fori_loop(0, 6, gone, 0)
+                out_ref[m, n, ri] = jnp.where(d == 0, d0, jnp.where(d == 1, d1, d2))
+    for n in range(3):
+        for kt in range(8):
+
+            @pl.when(away(n, kt))
+            def _():
+                third(n, kt).wait_send()
+    for b in range(6):
+        for ri in range(2):
+            core_copy(b, ri).wait_send()
+        for d in (1, 2, 3):
+            second(b, d).wait_send()
+            if by_rows(b):
+                rows_first(b, d, 0).wait_send()
+                rows_first(b, d, 1).wait_send()
+            else:
+                x_first(b, d).wait_send()
 
     def finish(i, _):
         for p in range(2):
@@ -569,18 +603,17 @@
             pltpu.VMEM((6, 2, 8, 2, 24, 384), F32),
             pltpu.VMEM((6, 2, 8, 24, 384), F32),
             pltpu.VMEM((6, 2, 4, 2, 24, 384), F32),
-            pltpu.VMEM((3, 3, 2, 2, 24, 384), F32),
-            pltpu.VMEM((3, 2, 2, 24, 384), F32),
-            pltpu.VMEM((3, 3, 4, 24, 384), F32),
-            pltpu.VMEM((3, 4, 24, 384), F32),
-            pltpu.VMEM((4, 6, 24, 128), F32),
-            pltpu.VMEM((3, 6, 24, 128), F32),
-            pltpu.VMEM((2, 6, 24, 128), F32),
+            pltpu.VMEM((4, 3, 2, 2, 24, 384), F32),
+            pltpu.VMEM((4, 2, 2, 24, 384), F32),
+            pltpu.VMEM((2, 3, 4, 24, 384), F32),
+            pltpu.VMEM((2, 4, 24, 384), F32),
+            pltpu.VMEM((3, 8, 24, 128), F32),
+            pltpu.VMEM((3, 8, 24, 128), F32),
             pltpu.VMEM((6, 3, 24, 384), F32),
             dma((16,)), dma((16,)), dma((2,)), dma((2,)),
             dma((2, 8)), dma((2, 8)), dma(()), dma(()),
-            dma((6,)), dma((6,)), dma((6, 3)), dma((6, 3)), dma((6, 3)), dma((6, 3)),
-            dma((3,)), dma((3,)), dma(()), dma(()),
+            dma((6, 2)), dma((6, 2)), dma((6, 6)), dma((6, 6)), dma((6, 3)), dma((6, 3)),
+            dma((3, 8)), dma((3, 8)),
         ],
         compiler_params=pltpu.CompilerParams(
             collective_id=0, has_side_effects=True, vmem_limit_bytes=60 << 20),

time: 124 us -> 112 us (0.903)
  Pallas kernels: 123 us -> 111 us
    pallas_call x1, Pallas kernels: 123 us -> 111 us  [elementals(): pl.pallas_call(kernel, out_shape=jax.ShapeDtypeStruct((2, 3, 2, 24, 48),...]
where the time goes in v4:
time: 112 us
  Pallas kernels  111 us (99%)
  local copies, waits for them, and re-layouts  1.58 us (1%)
    pallas_call x1, Pallas kernels, elementals(): pl.pallas_call(kernel, out_shape=jax.ShapeDtypeStruct((2, 3, 2, 24, 48),...  111 us

profile of v4, /device:TPU:0, one launch (start us, length us, event | category | flops | bytes accessed | tf_op | source)
XLA Modules:
  0.0 112.3 jit_solution(13167369819144906353)
XLA Ops:
  0.0 110.7 %elementals.1 = f32[2,3,2,24,48]{4,3,2,1,0:T(8,128)} custom-call(s32[2,3]{1,0:T(2,128)} %mom_ref.1, s32[3]{0:T(128)} %dir_ref.1, f32[4608,128]{1,0:T(8,128)} %bitcast.2, f32[864,128]{1,0:T(8,128)} %bitcast.3), custom_call_target="tpu_custom_call" | custom-call | flops 14269022208 | bytes 6291456 | tf_op jit(solution)/shard_map/elementals/pallas_call | solution.py:586
  110.7 1.6 %copy.6 = f32[2,3,2,24,48]{4,3,2,1,0:T(8,128)} copy(f32[2,3,2,24,48]{4,3,2,1,0:T(8,128)} %elementals.1) | data formatting | bytes 110592

commit v5 on v4

--- a/solution.py
+++ b/solution.py
@@ -47,8 +47,8 @@
     return out
 
 
-def kernel(mom_ref, dir_ref, x_ref, u_ref, out_ref,
-           stage, lstage, v_ref, up_ref, dn_ref, lk_ref, ulo_ref,
+def kernel(mom_ref, dir_ref, x_hbm, u_ref, out_ref,
+           x_ref, xsem, stage, lstage, v_ref, up_ref, dn_ref, lk_ref, ulo_ref,
            left, right02, right1, tab, e_ref, cin, cs, yin, ys, xin, xs, zst, zin, lin,
            send, recv, lsend, lrecv, fsend, frecv, usend, urecv,
            csend, crecv, asend, arecv, bsend, brecv, zsend, zrecv):
@@ -76,13 +76,16 @@
     s_next = (qn // 2 * 2 + xh) * 2 + qn % 2
     s_prev = (qp // 2 * 2 + xh) * 2 + qp % 2
 
-    def target(i):
-        xt, zt = (x + STEPS[i][0]) % 4, (z + STEPS[i][1]) % 4
+    def target(i, step=None):
+        dx, dz = STEPS[i] if step is None else step
+        xt, zt = (x + dx) % 4, (z + dz) % 4
         return (y * 2 + xt // 2) * 2 + xh, (xt % 2) * 4 + zt, xt * 4 + zt
 
     def origin(i):
         return (y * 2 + c) * 2 + i % 2, i // 2
 
+    fetch = pltpu.make_async_copy(x_hbm, x_ref, xsem)
+    fetch.start()
     barrier = pltpu.get_barrier_semaphore()
 
     def greet(i):
@@ -145,33 +148,52 @@
         def _():
             link_copy(xt).start()
 
-    lane = lane_of((144, 128))
-
-    def main_copy(i):
-        st, kt, j = target(i)
+
+    def main_copy(i, part, step=None):
+        st, kt, j = target(i, step)
+        r = pl.ds(part * 144, 144)
         return pltpu.make_async_remote_copy(
-            src_ref=stage.at[i], dst_ref=v_ref.at[c, k], send_sem=send.at[i],
-            recv_sem=recv.at[c * 8 + k], device_id=(st, kt), device_id_type=MESH)
-
-    def put(i):
-        st, kt, j = target(i)
-        nxt = (j + 1) % 16
-        stage[i, 0:288, :] = x_ref[pl.ds(j, 288, stride=16), :]
-        re = x_ref[pl.ds(nxt, 144, stride=16), :]
-        im = x_ref[pl.ds(144 * 16 + nxt, 144, stride=16), :]
-        stage[i, 288:432, :] = jnp.where(lane < 64, re, pltpu.roll(im, 64, 1))
+            src_ref=stage.at[i, r], dst_ref=v_ref.at[c, k, r], send_sem=send.at[part, i],
+            recv_sem=recv.at[part, c * 8 + k], device_id=(st, kt), device_id_type=MESH)
+
+    def arrived(p, vb, part):
+        r = pl.ds(part * 144, 144)
+        pltpu.make_async_copy(
+            v_ref.at[p, vb, r], v_ref.at[p, vb, r], recv.at[part, p * 8 + vb]).wait()
+
+    def put(i, part, step=None):
+        st, kt, j = target(i, step)
+        r = pl.ds(part * 144, 144)
+        if part < 2:
+            stage[i, r, :] = x_ref[pl.ds(part * 144 * 16 + j, 144, stride=16), :]
+        else:
+            nxt = (j + 1) % 16
+            re = x_ref[pl.ds(nxt, 144, stride=16), :]
+            im = x_ref[pl.ds(144 * 16 + nxt, 144, stride=16), :]
+            stage[i, r, :] = jnp.where(lane_of((144, 128)) < 64, re, pltpu.roll(im, 64, 1))
         mine = jnp.logical_and(st == s, kt == k)
 
         @pl.when(mine)
         def _():
-            pltpu.make_async_copy(stage.at[i], v_ref.at[c, k], recv.at[c * 8 + k]).start()
+            pltpu.make_async_copy(
+                stage.at[i, r], v_ref.at[c, k, r], recv.at[part, c * 8 + k]).start()
 
         @pl.when(jnp.logical_not(mine))
         def _():
-            main_copy(i).start()
-
+            main_copy(i, part, step).start()
+
+    fetch.wait()
     for i in range(16):
-        put(i)
+        put(i, 0)
+
+    packed_steps = tuple(
+        sum(STEPS[2 * n + odd][axis] * 4 ** n for n in range(8))
+        for odd in range(2) for axis in range(2))
+
+    def put_two(t, part, steps):
+        for odd in range(2):
+            put(2 * t + odd, part, (steps[2 * odd] % 4, steps[2 * odd + 1] % 4))
+        return tuple(n // 4 for n in steps)
 
     for p in range(2):
         pltpu.make_async_copy(lk_ref.at[p], lk_ref.at[p], lrecv.at[p]).wait()
@@ -180,11 +202,12 @@
         recv_sem=urecv, device_id=(s_next, k), device_id_type=MESH)
     ulo.start()
 
-    def hand(p, vb):
+    def hand(p, vb, part):
+        r = pl.ds(part * 144, 144)
         return pltpu.make_async_remote_copy(
-            src_ref=v_ref.at[p, vb, pl.ds(0, 288)],
-            dst_ref=(up_ref if p == 0 else dn_ref).at[vb],
-            send_sem=fsend.at[p, vb], recv_sem=frecv.at[p, vb],
+            src_ref=v_ref.at[p, vb, r],
+            dst_ref=(up_ref if p == 0 else dn_ref).at[vb, r],
+            send_sem=fsend.at[part, p, vb], recv_sem=frecv.at[part, p, vb],
             device_id=(s_prev if p == 0 else s_next, k), device_id_type=MESH)
 
     line = (xh * 2 + xl) * 4 + z
@@ -233,32 +256,52 @@
 
         return at, comp, link, put_right
 
+    def vectors_of(comp):
+        return [[(comp(v_ref, 0, cc, p), comp(v_ref, 1, cc, p)) for cc in range(3)] for p in range(2)]
+
+    def put_left(at, place, field):
+        for mm in range(2):
+            co, si = tab[mm, place, 0, 0:1], tab[mm, place, 1, 0:1]
+            for cc in range(3):
+                vr, vi = field[cc]
+                lr = vr * co - vi * si
+                li = -(vr * si + vi * co)
+                kk = pl.ds((6 + cc if place == 2 else cc * 2 + place) * 128, 128)
+                for i, t in enumerate((lr + li, lr, li)):
+                    hi, lo = halves(t)
+                    left[mm, i, 0, pl.ds(at, rows), kk] = hi
+                    left[mm, i, 1, pl.ds(at, rows), kk] = lo
+
     def inside(vb, sub):
         at, comp, link, put_right = tools(vb, sub)
-        v = [[(comp(v_ref, 0, cc, p), comp(v_ref, 1, cc, p)) for cc in range(3)] for p in range(2)]
+        v = vectors_of(comp)
+
+        def ahead(t):
+            return jnp.where(col == 63, pltpu.roll(t, 63, 1), pltpu.roll(t, 127, 1))
+
+        def behind(t):
+            return jnp.where(col == 0, pltpu.roll(t, 65, 1), pltpu.roll(t, 1, 1))
+
+        for p in range(2):
+            put_left(at, p, v[p])
+            fwd = apply_link(link(lk_ref, 2, False, p), [(ahead(a), ahead(b)) for a, b in v[p]])
+            bwd = apply_link(link(lk_ref, 2, True, p), v[p])
+            for cc in range(3):
+                put_right(2, p, cc, fwd[cc][0] - behind(bwd[cc][0]),
+                          fwd[cc][1] - behind(bwd[cc][1]))
+
+    def along(vb, sub):
+        at, comp, link, put_right = tools(vb, sub)
+        v = vectors_of(comp)
         packed = []
         for p in range(2):
             packed.append([
                 v_ref[p, vb, pl.ds(pl.multiple_of(288 + cc * 48 + sub * rows, rows), rows), :]
                 for cc in range(3)])
-        ext = [
+        put_left(at, 2, [
             (jnp.where(low, packed[0][cc], pltpu.roll(packed[1][cc], 64, 1)),
              jnp.where(low, pltpu.roll(packed[0][cc], 64, 1), packed[1][cc]))
-            for cc in range(3)]
-
-        for mm in range(2):
-            for place in range(3):
-                co, si = tab[mm, place, 0, 0:1], tab[mm, place, 1, 0:1]
-                for cc in range(3):
-                    vr, vi = ext[cc] if place == 2 else v[place][cc]
-                    lr = vr * co - vi * si
-                    li = -(vr * si + vi * co)
-                    kk = pl.ds((6 + cc if place == 2 else cc * 2 + place) * 128, 128)
-                    for i, t in enumerate((lr + li, lr, li)):
-                        hi, lo = halves(t)
-                        left[mm, i, 0, pl.ds(at, rows), kk] = hi
-                        left[mm, i, 1, pl.ds(at, rows), kk] = lo
-
+            for cc in range(3)])
         spill = []
         for p in range(2):
             shifted = []
@@ -276,17 +319,6 @@
                 put_right(1, p, cc, fwd[cc][0] - jnp.where(low, 0.0, tr),
                           fwd[cc][1] - jnp.where(low, 0.0, ti))
             spill.append((bwd, turned))
-            def ahead(t):
-                return jnp.where(col == 63, pltpu.roll(t, 63, 1), pltpu.roll(t, 127, 1))
-
-            def behind(t):
-                return jnp.where(col == 0, pltpu.roll(t, 65, 1), pltpu.roll(t, 1, 1))
-
-            fwd = apply_link(link(lk_ref, 2, False, p), [(ahead(a), ahead(b)) for a, b in v[p]])
-            bwd = apply_link(link(lk_ref, 2, True, p), v[p])
-            for cc in range(3):
-                put_right(2, p, cc, fwd[cc][0] - behind(bwd[cc][0]),
-                          fwd[cc][1] - behind(bwd[cc][1]))
         for cc in range(3):
             put_right(1, 2, cc,
                       -jnp.where(low, spill[0][1][cc][0], spill[1][0][cc][0]),
@@ -320,28 +352,54 @@
         digit = number % 8
         return digit // 4 * 4 + (z + 4 - digit % 4) % 4
 
-    def take(t, number):
+    def take_real(t, carry):
+        number, steps = carry
+        steps = put_two(t, 1, steps)
         vb = vector_block(number)
         for p in range(2):
-            pltpu.make_async_copy(v_ref.at[p, vb], v_ref.at[p, vb], recv.at[p * 8 + vb]).wait()
-            hand(p, vb).start()
+            arrived(p, vb, 0)
+            hand(p, vb, 0).start()
+        return number // 8, steps
+
+    def take(t, carry):
+        number, steps = carry
+        steps = put_two(t, 2, steps)
+        vb = vector_block(number)
+        for p in range(2):
+            arrived(p, vb, 1)
+            hand(p, vb, 1).start()
 
         def sub_loop(sub, _):
             inside(vb, sub)
             return 0
 
         lax.fori_loop(0, 3, sub_loop, 0)
-        return number // 8
-
-    lax.fori_loop(0, 8, take, arrivals(False))
+        return number // 8, steps
+
+    begin = arrivals(False), tuple(jnp.int32(n) for n in packed_steps)
+    lax.fori_loop(0, 8, take_real, begin)
+    lax.fori_loop(0, 8, take, begin)
 
     def join(t, number):
         vb = vector_block(number)
         for p in range(2):
-            hand(p, vb).wait_recv()
+            hand(p, vb, 0).wait_recv()
+            hand(p, vb, 1).wait_recv()
 
         def sub_loop(sub, _):
             across(vb, sub)
+            return 0
+
+        lax.fori_loop(0, 3, sub_loop, 0)
+        return number // 8
+
+    def late(t, number):
+        vb = vector_block(number)
+        for p in range(2):
+            arrived(p, vb, 2)
+
+        def sub_loop(sub, _):
+            along(vb, sub)
             return 0
 
         lax.fori_loop(0, 3, sub_loop, 0)
@@ -391,10 +449,10 @@
             src_ref=e_ref.at[b, ri, :, 1 - c], dst_ref=cin.at[b, ri], send_sem=csend.at[b, ri],
             recv_sem=crecv.at[b, ri], device_id=partner, device_id_type=MESH)
 
-    slot = {0: 0, 1: 1, 2: 2, 4: 3, 3: 0, 5: 1}
+    slot = {2: 0, 3: 1, 0: 2, 4: 3, 1: 0, 5: 1}
 
     def rows_first(b, d, ri):
-        at, to = (z, on_z) if b < 2 else (y, on_y)
+        at, to = (z, on_z) if b in (2, 3) else (y, on_y)
         return pltpu.make_async_remote_copy(
             src_ref=cs.at[b, ri, (at + d) % 4], dst_ref=yin.at[slot[b], d - 1, ri],
             send_sem=asend.at[b, 3 * ri + d - 1], recv_sem=arecv.at[b, 3 * ri + d - 1],
@@ -408,7 +466,7 @@
             device_id=on_x(d), device_id_type=MESH)
 
     def by_rows(b):
-        return b not in (3, 5)
+        return b not in (1, 5)
 
     def second(b, d):
         if by_rows(b):
@@ -421,13 +479,13 @@
             recv_sem=brecv.at[b, d - 1], device_id=to, device_id_type=MESH)
 
     def third(n, kt):
-        at = xl * 4 + y if n == 0 else k
+        at = xl * 4 + y if n == 1 else k
         return pltpu.make_async_remote_copy(
             src_ref=zst.at[n, kt], dst_ref=zin.at[n, at], send_sem=zsend.at[n, kt],
-            recv_sem=zrecv.at[n, at], device_id=(s_turned if n == 0 else s, kt), device_id_type=MESH)
+            recv_sem=zrecv.at[n, at], device_id=(s_turned if n == 1 else s, kt), device_id_type=MESH)
 
     def away(n, kt):
-        return jnp.logical_or(y != z, kt != k) if n == 0 else kt != k
+        return jnp.logical_or(y != z, kt != k) if n == 1 else kt != k
 
     def over_core(b, ri):
         core_copy(b, ri).wait_recv()
@@ -445,7 +503,7 @@
     def over_first(b):
         n = slot[b]
         if by_rows(b):
-            q = z if b < 2 else y
+            q = z if b in (2, 3) else y
             for ri in range(2):
                 for d in (1, 2, 3):
                     rows_first(b, d, ri).wait_recv()
@@ -478,7 +536,7 @@
             def _():
                 third(n, kt).start()
 
-        if n == 0:
+        if n == 1:
 
             @pl.when(y == z)
             def _():
@@ -486,12 +544,8 @@
         else:
             zin[n, k] = zst[n, k]
 
-    one_real(0)
-    one_imag(0)
-    over_core(0, 0)
     ulo.wait_recv()
     lax.fori_loop(0, 8, join, arrivals(True))
-    over_core(0, 1)
     pair_real(0)
     pair_imag(0)
     over_core(2, 0)
@@ -499,23 +553,28 @@
     pair_real(1)
     over_core(2, 1)
     over_core(3, 1)
-    over_first(0)
     pair_imag(1)
     over_core(4, 0)
     over_core(5, 0)
-    one_real(1)
+    lax.fori_loop(0, 8, late, arrivals(False))
     over_core(4, 1)
     over_core(5, 1)
+    one_real(0)
+    over_first(2)
+    over_first(3)
+    one_imag(0)
+    over_core(0, 0)
+    over_first(4)
+    over_first(5)
+    one_real(1)
+    over_core(0, 1)
+    over_second(1)
     one_imag(1)
     over_core(1, 0)
-    over_first(2)
-    over_first(3)
+    over_second(2)
     over_core(1, 1)
-    over_first(4)
-    over_first(5)
-    over_second(1)
+    over_first(0)
     over_first(1)
-    over_second(2)
     over_second(0)
 
     def arrive(n):
@@ -558,7 +617,8 @@
 
     def finish(i, _):
         for p in range(2):
-            hand(p, i).wait_send()
+            hand(p, i, 0).wait_send()
+            hand(p, i, 1).wait_send()
         return 0
 
     lax.fori_loop(0, 8, finish, 0)
@@ -574,7 +634,8 @@
 
         @pl.when(jnp.logical_or(st != s, kt != k))
         def _():
-            main_copy(i).wait_send()
+            for part in range(3):
+                main_copy(i, part).wait_send()
 
     for i in range(16):
         sent(i)
@@ -586,9 +647,11 @@
     return pl.pallas_call(
         kernel,
         out_shape=jax.ShapeDtypeStruct((2, 3, 2, 24, 48), F32),
-        in_specs=[smem, smem, VMEM, VMEM],
+        in_specs=[smem, smem, HBM, VMEM],
         out_specs=VMEM,
         scratch_shapes=[
+            pltpu.VMEM((288 * 16, 128), F32),
+            dma(()),
             pltpu.VMEM((16, 432, 128), F32),
             pltpu.VMEM((2, 56, 128), F32),
             pltpu.VMEM((2, 8, 432, 128), F32),
@@ -610,8 +673,8 @@
             pltpu.VMEM((3, 8, 24, 128), F32),
             pltpu.VMEM((3, 8, 24, 128), F32),
             pltpu.VMEM((6, 3, 24, 384), F32),
-            dma((16,)), dma((16,)), dma((2,)), dma((2,)),
-            dma((2, 8)), dma((2, 8)), dma(()), dma(()),
+            dma((3, 16)), dma((3, 16)), dma((2,)), dma((2,)),
+            dma((2, 2, 8)), dma((2, 2, 8)), dma(()), dma(()),
             dma((6, 2)), dma((6, 2)), dma((6, 6)), dma((6, 6)), dma((6, 3)), dma((6, 3)),
             dma((3, 8)), dma((3, 8)),
         ],

time: 112 us -> 105 us (0.938)
  Pallas kernels: 111 us -> 103 us
    pallas_call x1, Pallas kernels: 111 us -> 103 us  [elementals(): pl.pallas_call(kernel, out_shape=jax.ShapeDtypeStruct((2, 3, 2, 24, 48),...]
where the time goes in v5:
time: 105 us
  Pallas kernels  103 us (98%)
  local copies, waits for them, and re-layouts  1.58 us (2%)
    pallas_call x1, Pallas kernels, elementals(): pl.pallas_call(kernel, out_shape=jax.ShapeDtypeStruct((2, 3, 2, 24, 48),...  103 us

profile of v5, /device:TPU:0, one launch (start us, length us, event | category | flops | bytes accessed | tf_op | source)
XLA Modules:
  0.0 104.5 jit_solution(9206963031840860153)
XLA Ops:
  0.0 102.9 %elementals.1 = f32[2,3,2,24,48]{4,3,2,1,0:T(8,128)} custom-call(s32[2,3]{1,0:T(2,128)} %mom_ref.1, s32[3]{0:T(128)} %dir_ref.1, f32[4608,128]{1,0:T(8,128)} %bitcast.2, f32[864,128]{1,0:T(8,128)} %bitcast.3), custom_call_target="tpu_custom_call" | custom-call | flops 14269022208 | bytes 6291456 | tf_op jit(solution)/shard_map/elementals/pallas_call | solution.py:647
  102.9 1.6 %copy.6 = f32[2,3,2,24,48]{4,3,2,1,0:T(8,128)} copy(f32[2,3,2,24,48]{4,3,2,1,0:T(8,128)} %elementals.1) | data formatting | bytes 110592

commit v6 on v5

--- a/solution.py
+++ b/solution.py
@@ -23,8 +23,8 @@
     return lax.broadcasted_iota(jnp.int32, shape, len(shape) - 1)
 
 
-STEPS = ((2, 2), (1, 2), (3, 2), (2, 1), (2, 3), (1, 1), (3, 3), (1, 3),
-         (3, 1), (2, 0), (0, 2), (0, 1), (0, 3), (1, 0), (3, 0), (0, 0))
+STEPS = ((1, 0), (0, 1), (3, 0), (0, 3), (2, 0), (0, 2), (1, 1), (3, 3),
+         (1, 3), (3, 1), (1, 2), (2, 1), (3, 2), (2, 3), (2, 2), (0, 0))
 
 
 def halves(t):
@@ -560,20 +560,20 @@
     over_core(4, 1)
     over_core(5, 1)
     one_real(0)
+    one_imag(0)
+    over_core(0, 0)
     over_first(2)
     over_first(3)
-    one_imag(0)
-    over_core(0, 0)
+    one_real(1)
+    over_core(0, 1)
     over_first(4)
     over_first(5)
-    one_real(1)
-    over_core(0, 1)
-    over_second(1)
     one_imag(1)
     over_core(1, 0)
+    over_core(1, 1)
+    over_second(1)
+    over_first(0)
     over_second(2)
-    over_core(1, 1)
-    over_first(0)
     over_first(1)
     over_second(0)
 

time: 105 us -> 99.9 us (0.951)
  Pallas kernels: 103 us -> 98.1 us
    pallas_call x1, Pallas kernels: 103 us -> 98.1 us  [elementals(): pl.pallas_call(kernel, out_shape=jax.ShapeDtypeStruct((2, 3, 2, 24, 48),...]
where the time goes in v6:
time: 99.9 us; the launch traced here: 99.7 us
  Pallas kernels  98.1 us (98%)
  local copies, waits for them, and re-layouts  1.58 us (2%)
    pallas_call x1, Pallas kernels, elementals(): pl.pallas_call(kernel, out_shape=jax.ShapeDtypeStruct((2, 3, 2, 24, 48),...  98.1 us

profile of v6, /device:TPU:0, one launch (start us, length us, event | category | flops | bytes accessed | tf_op | source)
XLA Modules:
  0.0 99.7 jit_solution(1892925773218824230)
XLA Ops:
  0.0 98.1 %elementals.1 = f32[2,3,2,24,48]{4,3,2,1,0:T(8,128)} custom-call(s32[2,3]{1,0:T(2,128)} %mom_ref.1, s32[3]{0:T(128)} %dir_ref.1, f32[4608,128]{1,0:T(8,128)} %bitcast.2, f32[864,128]{1,0:T(8,128)} %bitcast.3), custom_call_target="tpu_custom_call" | custom-call | flops 14269022208 | bytes 6291456 | tf_op jit(solution)/shard_map/elementals/pallas_call | solution.py:647
  98.1 1.6 %copy.6 = f32[2,3,2,24,48]{4,3,2,1,0:T(8,128)} copy(f32[2,3,2,24,48]{4,3,2,1,0:T(8,128)} %elementals.1) | data formatting | bytes 110592

commit v7 on v6

--- a/solution.py
+++ b/solution.py
@@ -363,11 +363,11 @@
 
     def take(t, carry):
         number, steps = carry
-        steps = put_two(t, 2, steps)
         vb = vector_block(number)
         for p in range(2):
             arrived(p, vb, 1)
             hand(p, vb, 1).start()
+        steps = put_two(t, 2, steps)
 
         def sub_loop(sub, _):
             inside(vb, sub)
@@ -570,9 +570,9 @@
     over_first(5)
     one_imag(1)
     over_core(1, 0)
+    over_first(0)
     over_core(1, 1)
     over_second(1)
-    over_first(0)
     over_second(2)
     over_first(1)
     over_second(0)

time: 99.9 us -> 102 us (1.021)
  Pallas kernels: 98.1 us -> 101 us
    pallas_call x1, Pallas kernels: 98.1 us -> 101 us  [elementals(): pl.pallas_call(kernel, out_shape=jax.ShapeDtypeStruct((2, 3, 2, 24, 48),...]
where the time goes in v7:
time: 102 us
  Pallas kernels  101 us (99%)
  local copies, waits for them, and re-layouts  1.58 us (2%)
    pallas_call x1, Pallas kernels, elementals(): pl.pallas_call(kernel, out_shape=jax.ShapeDtypeStruct((2, 3, 2, 24, 48),...  101 us

profile of v7, /device:TPU:0, one launch (start us, length us, event | category | flops | bytes accessed | tf_op | source)
XLA Modules:
  0.0 102.2 jit_solution(5458902680837027834)
XLA Ops:
  0.0 100.7 %elementals.1 = f32[2,3,2,24,48]{4,3,2,1,0:T(8,128)} custom-call(s32[2,3]{1,0:T(2,128)} %mom_ref.1, s32[3]{0:T(128)} %dir_ref.1, f32[4608,128]{1,0:T(8,128)} %bitcast.2, f32[864,128]{1,0:T(8,128)} %bitcast.3), custom_call_target="tpu_custom_call" | custom-call | flops 14269022208 | bytes 6291456 | tf_op jit(solution)/shard_map/elementals/pallas_call | solution.py:647
  100.7 1.6 %copy.6 = f32[2,3,2,24,48]{4,3,2,1,0:T(8,128)} copy(f32[2,3,2,24,48]{4,3,2,1,0:T(8,128)} %elementals.1) | data formatting | bytes 110592
